TPU v7x, 32 devices: a whole 2x2x4 slice. The times are simulated.
32 devices in a mesh: seq: 2 (over x), ctx: 4 (over z), fsdp: 4 (over y, core).
Axes of the slice: x: 2, y: 2, z: 4, core: 2. Of those that a mesh axis runs over, the one named last changes fastest.
Arguments:
- hidden: bfloat16 [8, 1024, 1024], P(('seq', 'fsdp'), 'ctx'), may hold values from -6 to 6
- encoder: bfloat16 [8, 256, 1024], P(('seq', 'fsdp'), 'ctx'), may hold values from -6 to 6
- attn_qkv: bfloat16 [1024, 3072], P('fsdp'), may hold values from -0.1875 to 0.1875
- attn_out: bfloat16 [1024, 1024], P('fsdp'), may hold values from -0.5 to 0.5
- cross_q: bfloat16 [1024, 1024], P('fsdp'), may hold values from -0.1875 to 0.1875
- cross_kv: bfloat16 [1024, 2048], P('fsdp'), may hold values from -0.1875 to 0.1875
- cross_out: bfloat16 [1024, 1024], P('fsdp'), may hold values from -0.5 to 0.5
- ff_in: bfloat16 [1024, 4096], P('fsdp'), may hold values from -0.1875 to 0.1875
- ff_out: bfloat16 [4096, 1024], P('fsdp'), may hold values from -0.09375 to 0.09375
- norm_gains: bfloat16 [3, 1024], P(None, 'fsdp'), may hold values from 0.5 to 1.5
- norm_biases: bfloat16 [3, 1024], P(None, 'fsdp'), may hold values from -3 to 3
- block_table: int32 [4, 2], replicated, may hold values from 0 to 7, as said below
- out_grad: bfloat16 [8, 1024, 1024], P(('seq', 'fsdp'), 'ctx'), may hold values from -6 to 6
Outputs:
- mixed: bfloat16 [8, 1024, 1024], P(('seq', 'fsdp'), 'ctx')
- grad_input: float32 [8, 1024, 1024], P(('seq', 'fsdp'), 'ctx')
- grad_encoder: float32 [8, 256, 1024], P(('seq', 'fsdp'), 'ctx')
- grad_attn_qkv: float32 [1024, 3072], P('fsdp')
- grad_attn_out: float32 [1024, 1024], P('fsdp')
- grad_cross_q: float32 [1024, 1024], P('fsdp')
- grad_cross_kv: float32 [1024, 2048], P('fsdp')
- grad_cross_out: float32 [1024, 1024], P('fsdp')
- grad_ff_in: float32 [1024, 4096], P('fsdp')
- grad_ff_out: float32 [4096, 1024], P('fsdp')
- grad_norm_gains: float32 [3, 1024], P(None, 'fsdp')
- grad_norm_biases: float32 [3, 1024], P(None, 'fsdp')
Inputs may be any that keep to these rules, and one draw needn't show every extreme that they name: `block_table`: row c holds two blocks b and 7 - b in either order; every block number of one sequence appears exactly once in the table.
All inputs are finite; a program needn't handle non-finite values.
Results may differ from a plain program's by a relative error of at most 0.023.
Values may be sent and summed in bfloat16 or wider, within the bound.
No kernel may reach another device: no remote copies, remote signals or barrier semaphores. Data moves between devices by JAX's collectives and lax.ppermute only.
A program may use at most 256 MiB of HBM per device.

v0:
```python
import math

import jax
import jax.numpy as jnp
from jax import lax
from jax.sharding import PartitionSpec as P

HEADS = 16
HEAD_DIM = 64


def matmul(left, right):
    return jnp.dot(left, right, preferred_element_type=jnp.float32)


def over_rows(left, right):
    return lax.dot_general(
        left, right, (((0,), (0,)), ((), ())), preferred_element_type=jnp.float32
    )


def against(left, right):
    return lax.dot_general(
        left, right, (((1,), (1,)), ((), ())), preferred_element_type=jnp.float32
    )


def layer_norm(value, gain, shift):
    centre = jnp.mean(value, -1, keepdims=True)
    centred = value - centre
    spread = jnp.mean(centred * centred, -1, keepdims=True)
    return centred * lax.rsqrt(spread + 1e-05) * gain + shift


def gelu_exact(value):
    return jax.nn.gelu(value, approximate=False)


def key_block(keyval, index, size, heads):
    piece = lax.dynamic_slice_in_dim(keyval, index * size, size, 1)
    half = piece.shape[2] // 2
    keys = piece[:, :, :half].reshape(piece.shape[0], size, heads, half // heads)
    values = piece[:, :, half:].reshape(piece.shape[0], size, heads, half // heads)
    return (keys, values)


def block_scores(query, keys, query_pos, key_pos, index, size):
    scores = jnp.einsum(
        "srhd,skhd->shrk", query, keys, preferred_element_type=jnp.float32
    ) * HEAD_DIM ** (-0.5)
    if query_pos is None:
        return (scores, None)
    here = lax.dynamic_slice_in_dim(key_pos, index * size, size, 0)
    allowed = here[None, :] <= query_pos[:, None]
    return (jnp.where(allowed, scores, -1e30), allowed)


def mask_probs(values, allowed):
    if allowed is None:
        return values
    return jnp.where(allowed, values, 0.0)


def attend_forward(query, keyval, query_pos, key_pos, heads):
    seqs, rows, depth = (query.shape[0], query.shape[1], query.shape[3])
    size = math.gcd(keyval.shape[1], 512)
    count = keyval.shape[1] // size

    def gather_stats(carry, index):
        top, total = carry
        keys, values = key_block(keyval, index, size, heads)
        scores, allowed = block_scores(query, keys, query_pos, key_pos, index, size)
        new_top = jnp.maximum(top, jnp.max(scores, -1))
        expo = mask_probs(jnp.exp(scores - new_top[..., None]), allowed)
        return ((new_top, total * jnp.exp(top - new_top) + jnp.sum(expo, -1)), None)

    start = (
        jnp.full((seqs, heads, rows), -1e30, jnp.float32),
        jnp.zeros((seqs, heads, rows), jnp.float32),
    )
    (top, total), unused = lax.scan(gather_stats, start, jnp.arange(count))
    log_total = top + jnp.log(total)

    def weigh(accum, index):
        keys, values = key_block(keyval, index, size, heads)
        scores, allowed = block_scores(query, keys, query_pos, key_pos, index, size)
        probs = mask_probs(jnp.exp(scores - log_total[..., None]), allowed).astype(jnp.bfloat16)
        return (
            accum
            + jnp.einsum("shrk,skhd->srhd", probs, values, preferred_element_type=jnp.float32),
            None,
        )

    output, unused = lax.scan(
        weigh, jnp.zeros((seqs, rows, heads, depth), jnp.float32), jnp.arange(count)
    )
    return (output, log_total)


def attend_backward(query, keyval, query_pos, key_pos, output, log_total, d_output, heads):
    seqs, rows, depth = (query.shape[0], query.shape[1], query.shape[3])
    size = math.gcd(keyval.shape[1], 512)
    count = keyval.shape[1] // size
    scale = HEAD_DIM ** (-0.5)
    delta = jnp.einsum("srhd,srhd->shr", d_output.astype(jnp.float32), output)

    def step(carry, index):
        d_query, d_keyval = carry
        keys, values = key_block(keyval, index, size, heads)
        scores, allowed = block_scores(query, keys, query_pos, key_pos, index, size)
        probs = mask_probs(jnp.exp(scores - log_total[..., None]), allowed)
        d_values = jnp.einsum(
            "shrk,srhd->skhd",
            probs.astype(jnp.bfloat16),
            d_output,
            preferred_element_type=jnp.float32,
        )
        d_probs = jnp.einsum(
            "srhd,skhd->shrk", d_output, values, preferred_element_type=jnp.float32
        )
        d_scores = (probs * (d_probs - delta[..., None])).astype(jnp.bfloat16)
        d_query = (
            d_query
            + jnp.einsum("shrk,skhd->srhd", d_scores, keys, preferred_element_type=jnp.float32)
            * scale
        )
        d_keys = (
            jnp.einsum("shrk,srhd->skhd", d_scores, query, preferred_element_type=jnp.float32)
            * scale
        )
        piece = jnp.concatenate(
            [
                d_keys.reshape(seqs, size, heads * depth),
                d_values.reshape(seqs, size, heads * depth),
            ],
            -1,
        )
        return ((d_query, lax.dynamic_update_slice_in_dim(d_keyval, piece, index * size, 1)), None)

    start = (
        jnp.zeros((seqs, rows, heads, depth), jnp.float32),
        jnp.zeros(keyval.shape, jnp.float32),
    )
    (d_query, d_keyval), unused = lax.scan(step, start, jnp.arange(count))
    return (d_query, d_keyval)


def local(
    hidden,
    encoder,
    attn_qkv,
    attn_out,
    cross_q,
    cross_kv,
    cross_out,
    ff_in,
    ff_out,
    norm_gains,
    norm_biases,
    block_table,
    out_grad,
):
    seqs, rows, width = hidden.shape
    heads = HEADS
    depth = width // heads
    enc_rows = encoder.shape[1]
    matrices = (attn_qkv, attn_out, cross_q, cross_kv, cross_out, ff_in, ff_out)
    full = (
        lax.all_gather(attn_qkv, "fsdp", axis=0, tiled=True),
        lax.all_gather(attn_out, "fsdp", axis=0, tiled=True),
        lax.all_gather(cross_q, "fsdp", axis=0, tiled=True),
        lax.all_gather(cross_kv, "fsdp", axis=0, tiled=True),
        lax.all_gather(cross_out, "fsdp", axis=0, tiled=True),
        lax.all_gather(ff_in, "fsdp", axis=0, tiled=True),
        lax.all_gather(ff_out, "fsdp", axis=0, tiled=True),
        lax.all_gather(norm_gains, "fsdp", axis=1, tiled=True),
        lax.all_gather(norm_biases, "fsdp", axis=1, tiled=True),
    )
    wqkv, wout_self, wcq, wckv, wco, wfin, wfout = full[:7]
    gains = full[7].astype(jnp.float32)
    shifts = full[8].astype(jnp.float32)
    half_rows = rows // 2
    place = lax.axis_index("ctx")
    mine = lax.dynamic_index_in_dim(block_table, place, 0, keepdims=False)
    offsets = jnp.arange(half_rows, dtype=jnp.int32)
    query_pos = (mine[:, None] * half_rows + offsets[None, :]).reshape(rows)
    key_pos = (block_table[:, :, None] * half_rows + offsets[None, None, :]).reshape(-1)
    flat = hidden.reshape(seqs * rows, width)
    qkv = matmul(flat, wqkv).astype(jnp.bfloat16).reshape(seqs, rows, 3 * width)
    query = qkv[:, :, :width].reshape(seqs, rows, heads, depth)
    keyval = qkv[:, :, width:]
    keys_all = lax.all_gather(keyval, "ctx", axis=1, tiled=True)
    self_output, self_total = attend_forward(query, keys_all, query_pos, key_pos, heads)
    self_low = self_output.astype(jnp.bfloat16).reshape(seqs * rows, width)
    resid_one = flat.astype(jnp.float32) + matmul(self_low, wout_self)
    first = layer_norm(resid_one, gains[0], shifts[0])
    first_low = first.astype(jnp.bfloat16)
    cross_query = matmul(first_low, wcq).astype(jnp.bfloat16).reshape(seqs, rows, heads, depth)
    enc_flat = encoder.reshape(seqs * enc_rows, width)
    enc_keyval = matmul(enc_flat, wckv).astype(jnp.bfloat16).reshape(seqs, enc_rows, 2 * width)
    enc_all = lax.all_gather(enc_keyval, "ctx", axis=1, tiled=True)
    cross_output, cross_total = attend_forward(cross_query, enc_all, None, None, heads)
    cross_low = cross_output.astype(jnp.bfloat16).reshape(seqs * rows, width)
    resid_two = first + matmul(cross_low, wco)
    second = layer_norm(resid_two, gains[1], shifts[1])
    second_low = second.astype(jnp.bfloat16)
    pre = matmul(second_low, wfin)
    act = gelu_exact(pre).astype(jnp.bfloat16)
    resid_three = second + matmul(act, wfout)
    mixed = (
        layer_norm(resid_three, gains[2], shifts[2]).astype(jnp.bfloat16).reshape(seqs, rows, width)
    )
    wqkv, wout_self, wcq, wckv, wco, wfin, wfout = (
        lax.all_gather(matrices[0], "fsdp", axis=0, tiled=True),
        lax.all_gather(matrices[1], "fsdp", axis=0, tiled=True),
        lax.all_gather(matrices[2], "fsdp", axis=0, tiled=True),
        lax.all_gather(matrices[3], "fsdp", axis=0, tiled=True),
        lax.all_gather(matrices[4], "fsdp", axis=0, tiled=True),
        lax.all_gather(matrices[5], "fsdp", axis=0, tiled=True),
        lax.all_gather(matrices[6], "fsdp", axis=0, tiled=True),
    )
    d_out = out_grad.reshape(seqs * rows, width).astype(jnp.float32)
    unused, pull_three = jax.vjp(layer_norm, resid_three, gains[2], shifts[2])
    d_resid_three, d_gain_three, d_shift_three = pull_three(d_out)
    d_ffo = d_resid_three.astype(jnp.bfloat16)
    grad_ff_out = over_rows(act, d_ffo)
    d_act = against(d_ffo, wfout)
    unused, pull_gelu = jax.vjp(gelu_exact, pre)
    d_pre = pull_gelu(d_act)[0].astype(jnp.bfloat16)
    grad_ff_in = over_rows(second_low, d_pre)
    d_second = d_resid_three + against(d_pre, wfin)
    unused, pull_two = jax.vjp(layer_norm, resid_two, gains[1], shifts[1])
    d_resid_two, d_gain_two, d_shift_two = pull_two(d_second)
    d_cross = d_resid_two.astype(jnp.bfloat16)
    grad_cross_out = over_rows(cross_low, d_cross)
    d_cat = against(d_cross, wco).astype(jnp.bfloat16).reshape(seqs, rows, heads, depth)
    d_cross_query, d_enc_terms = attend_backward(
        cross_query, enc_all, None, None, cross_output, cross_total, d_cat, heads
    )
    d_enc_keyval = lax.psum_scatter(
        d_enc_terms.astype(jnp.bfloat16), "ctx", scatter_dimension=1, tiled=True
    ).reshape(seqs * enc_rows, 2 * width)
    grad_cross_kv = over_rows(enc_flat, d_enc_keyval)
    grad_encoder = against(d_enc_keyval, wckv).reshape(seqs, enc_rows, width)
    d_cq_low = d_cross_query.astype(jnp.bfloat16).reshape(seqs * rows, width)
    grad_cross_q = over_rows(first_low, d_cq_low)
    d_first = d_resid_two + against(d_cq_low, wcq)
    unused, pull_one = jax.vjp(layer_norm, resid_one, gains[0], shifts[0])
    d_resid_one, d_gain_one, d_shift_one = pull_one(d_first)
    d_attn = d_resid_one.astype(jnp.bfloat16)
    grad_attn_out = over_rows(self_low, d_attn)
    d_self = against(d_attn, wout_self).astype(jnp.bfloat16).reshape(seqs, rows, heads, depth)
    keys_back = lax.all_gather(keyval, "ctx", axis=1, tiled=True)
    d_query, d_kv_terms = attend_backward(
        query, keys_back, query_pos, key_pos, self_output, self_total, d_self, heads
    )
    d_keyval = lax.psum_scatter(
        d_kv_terms.astype(jnp.bfloat16), "ctx", scatter_dimension=1, tiled=True
    )
    d_qkv = jnp.concatenate(
        [d_query.astype(jnp.bfloat16).reshape(seqs, rows, width), d_keyval], -1
    ).reshape(seqs * rows, 3 * width)
    grad_attn_qkv = over_rows(flat, d_qkv)
    grad_input = (d_resid_one + against(d_qkv, wqkv)).reshape(seqs, rows, width)
    gain_terms = jnp.stack([d_gain_one, d_gain_two, d_gain_three])
    shift_terms = jnp.stack([d_shift_one, d_shift_two, d_shift_three])
    shards = (
        lax.psum_scatter(
            grad_attn_qkv.astype(jnp.bfloat16), "fsdp", scatter_dimension=0, tiled=True
        ).astype(jnp.float32),
        lax.psum_scatter(
            grad_attn_out.astype(jnp.bfloat16), "fsdp", scatter_dimension=0, tiled=True
        ).astype(jnp.float32),
        lax.psum_scatter(
            grad_cross_q.astype(jnp.bfloat16), "fsdp", scatter_dimension=0, tiled=True
        ).astype(jnp.float32),
        lax.psum_scatter(
            grad_cross_kv.astype(jnp.bfloat16), "fsdp", scatter_dimension=0, tiled=True
        ).astype(jnp.float32),
        lax.psum_scatter(
            grad_cross_out.astype(jnp.bfloat16), "fsdp", scatter_dimension=0, tiled=True
        ).astype(jnp.float32),
        lax.psum_scatter(
            grad_ff_in.astype(jnp.bfloat16), "fsdp", scatter_dimension=0, tiled=True
        ).astype(jnp.float32),
        lax.psum_scatter(
            grad_ff_out.astype(jnp.bfloat16), "fsdp", scatter_dimension=0, tiled=True
        ).astype(jnp.float32),
        lax.psum_scatter(
            gain_terms.astype(jnp.bfloat16), "fsdp", scatter_dimension=1, tiled=True
        ).astype(jnp.float32),
        lax.psum_scatter(
            shift_terms.astype(jnp.bfloat16), "fsdp", scatter_dimension=1, tiled=True
        ).astype(jnp.float32),
    )
    totals = (
        lax.psum(shards[0].astype(jnp.bfloat16), ("seq", "ctx")).astype(jnp.float32),
        lax.psum(shards[1].astype(jnp.bfloat16), ("seq", "ctx")).astype(jnp.float32),
        lax.psum(shards[2].astype(jnp.bfloat16), ("seq", "ctx")).astype(jnp.float32),
        lax.psum(shards[3].astype(jnp.bfloat16), ("seq", "ctx")).astype(jnp.float32),
        lax.psum(shards[4].astype(jnp.bfloat16), ("seq", "ctx")).astype(jnp.float32),
        lax.psum(shards[5].astype(jnp.bfloat16), ("seq", "ctx")).astype(jnp.float32),
        lax.psum(shards[6].astype(jnp.bfloat16), ("seq", "ctx")).astype(jnp.float32),
        lax.psum(shards[7].astype(jnp.bfloat16), ("seq", "ctx")).astype(jnp.float32),
        lax.psum(shards[8].astype(jnp.bfloat16), ("seq", "ctx")).astype(jnp.float32),
    )
    return (
        mixed,
        grad_input,
        grad_encoder,
        totals[0],
        totals[1],
        totals[2],
        totals[3],
        totals[4],
        totals[5],
        totals[6],
        totals[7],
        totals[8],
    )


def solution(mesh):
    in_specs = (
        P(("seq", "fsdp"), "ctx", None),
        P(("seq", "fsdp"), "ctx", None),
        P("fsdp", None),
        P("fsdp", None),
        P("fsdp", None),
        P("fsdp", None),
        P("fsdp", None),
        P("fsdp", None),
        P("fsdp", None),
        P(None, "fsdp"),
        P(None, "fsdp"),
        P(),
        P(("seq", "fsdp"), "ctx", None),
    )
    out_specs = (
        P(("seq", "fsdp"), "ctx", None),
        P(("seq", "fsdp"), "ctx", None),
        P(("seq", "fsdp"), "ctx", None),
        P("fsdp", None),
        P("fsdp", None),
        P("fsdp", None),
        P("fsdp", None),
        P("fsdp", None),
        P("fsdp", None),
        P("fsdp", None),
        P(None, "fsdp"),
        P(None, "fsdp"),
    )
    return jax.shard_map(local, mesh=mesh, in_specs=in_specs, out_specs=out_specs, check_vma=False)
```

profile of v0, /device:TPU:0, one launch (start us, length us, event | category | flops | bytes accessed | tf_op | source)
XLA Modules:
  0.0 1277.5 jit_solution(1041879794882100429)
XLA Ops:
  8.7 38.1 %all-gather.17.cloned.1.call-done = bf16[1024,2048]{1,0:T(8,128)(2,1)} async-done(((bf16[256,2048]{1,0:T(8,128)(2,1)}), bf16[1024,2048]{1,0:T(8,128)(2,1)}) %all-gather.17.cloned.1.call-update) | async-done | bytes 4194320 | tf_op jit(solution)/shard_map/all_gather | solution.py:172
  50.6 44.2 %all-gather.11.cloned.1.call-done = bf16[1024,3072]{1,0:T(8,128)(2,1)} async-done(((bf16[256,3072]{1,0:T(8,128)(2,1)}), bf16[1024,3072]{1,0:T(8,128)(2,1)}) %all-gather.11.cloned.1.call-update) | async-done | bytes 6291472 | tf_op jit(solution)/shard_map/all_gather | solution.py:169
  116.1 8.8 all-gather.27.cloned.1.call-done
  128.9 78.3 %all-gather.13.cloned.1.call-done = bf16[1,1024,2048]{2,1,0:T(8,128)(2,1)} async-done(((bf16[1,256,2048]{2,1,0:T(8,128)(2,1)}), bf16[1,1024,2048]{2,1,0:T(8,128)(2,1)}) %all-gather.13.cloned.1.call-update) | async-done | bytes 4194320 | tf_op jit(solution)/shard_map/all_gather | solution.py:192
  213.6 24.3 %while.9 = (s32[]{:T(128)}, f32[1,16,256]{2,1,0:T(8,128)S(1)}, f32[1,16,256]{2,1,0:T(8,128)S(1)}, s32[2]{0:T(128)S(1)}, s32[1024]{0:T(1024)S(1)}, /*index=5*/bf1...) while((s32[]{:T(128)}, f32[1,16,256]{2,1,0:T(8,128)S(1)}, ...), condition=%wide.region_3.4_spmd.clone, body=%wide.region_0.3_spmd.clone.sunk | while | flops 285364480 | bytes 21061832 | solution.py:81
  237.9 15.4 %while.10 = (s32[]{:T(128)}, f32[1,256,16,64]{1,3,2,0:T(8,128)}, s32[2]{0:T(128)S(1)}, bf16[1,1024,2048]{1,2,0:T(8,128)(2,1)}, s32[1024]{0:T(1024)S(1)}, /*index...) while((s32[]{:T(128)}, f32[1,256,16,64]{1,3,2,0:T(8,128)}, ...), condition=%wide.region_5.6_spmd.clone, body=%wide.region_4.5_spmd.clone.sunk | while | flops 548012288 | bytes 9199841 | solution.py:94
  268.7 9.3 all-gather.21.cloned.1.call-done
  280.9 57.0 %all-gather.23.cloned.1.call-done = bf16[1024,4096]{1,0:T(8,128)(2,1)} async-done(((bf16[256,4096]{1,0:T(8,128)(2,1)}), bf16[1024,4096]{1,0:T(8,128)(2,1)}) %all-gather.23.cloned.1.call-update) | async-done | bytes 8388624 | tf_op jit(solution)/shard_map/all_gather | solution.py:174
  337.9 16.2 %multiply_convert_fusion.1 = (bf16[256,4096]{1,0:T(8,128)(2,1)}, f32[256,4096]{1,0:T(8,128)}, f32[256,4096]{1,0:T(8,128)}) fusion(bf16[1024,4096]{1,0:T(8,128)(2,1)} %all-gather.23.cloned.1.call-done, f32[256,1024]{1,0:T(8,128)S(1)} %get-tuple-element.531, f32[1024]{0:T(1024)S(1)} %bitcast.384, f32[1024]{0:T(1024)S(1)} %bitcast.374, f32[256]{0:T(256)S(1)} %fusion.77, ...), kind=kOutput, calls=%fused_computation.66 | convolution fusion | flops 2216951808 | bytes 19933184 | tf_op jit(solution)/shard_map/dot_general | solution.py:13
  354.1 43.7 %all-gather.25.cloned.1.call-done = bf16[4096,1024]{1,0:T(8,128)(2,1)} async-done(((bf16[1024,1024]{1,0:T(8,128)(2,1)}), bf16[4096,1024]{1,0:T(8,128)(2,1)}) %all-gather.25.cloned.1.call-update) | async-done | bytes 8388624 | tf_op jit(solution)/shard_map/all_gather | solution.py:175
  406.9 11.2 add_convert_fusion
  452.9 37.8 %while.11 = (s32[]{:T(128)}, f32[1,256,16,64]{1,3,2,0:T(8,128)}, bf16[1,1024,2048]{1,2,0:T(8,128)(2,1)}, s32[2]{0:T(128)S(1)}, bf16[1,1024,2048]{1,2,0:T(8,128)(...) while((s32[]{:T(128)}, f32[1,256,16,64]{1,3,2,0:T(8,128)}, ...), condition=%wide.region_21.22_spmd.clone, body=%wide.region_20.21_spmd.clone.sunk | while | flops 1373503744 | bytes 72802584 | solution.py:144
  523.7 44.0 %reduce-scatter.18.cloned.1.call-done = bf16[1,256,2048]{1,2,0:T(8,128)(2,1)} async-done(((bf16[1,1024,2048]{1,2,0:T(8,128)(2,1)}), bf16[1,256,2048]{1,2,0:T(8,128)(2,1)}) %reduce-scatter.18.cloned.1.call-update) | async-done | bytes 1048592 | tf_op jit(solution)/shard_map/reduce_scatter | solution.py:257
  576.6 25.5 %reduce-scatter.28.cloned.1.call-done = bf16[256,1024]{1,0:T(8,128)(2,1)} async-done(((bf16[1024,1024]{1,0:T(8,128)(2,1)}), bf16[256,1024]{1,0:T(8,128)(2,1)}) %reduce-scatter.28.cloned.1.call-update) | async-done | bytes 524304 | tf_op jit(solution)/shard_map/reduce_scatter | solution.py:280
  602.1 34.2 %reduce-scatter.24.cloned.1.call-done = bf16[256,1024]{1,0:T(8,128)(2,1)} async-done(((bf16[1024,1024]{1,0:T(8,128)(2,1)}), bf16[256,1024]{1,0:T(8,128)(2,1)}) %reduce-scatter.24.cloned.1.call-update) | async-done | bytes 524304 | tf_op jit(solution)/shard_map/reduce_scatter | solution.py:274
  636.2 34.4 %reduce-scatter.22.cloned.1.call-done = bf16[256,1024]{1,0:T(8,128)(2,1)} async-done(((bf16[1024,1024]{1,0:T(8,128)(2,1)}), bf16[256,1024]{1,0:T(8,128)(2,1)}) %reduce-scatter.22.cloned.1.call-update) | async-done | bytes 524304 | tf_op jit(solution)/shard_map/reduce_scatter | solution.py:271
  670.6 47.7 %reduce-scatter.26.cloned.1.call-done = bf16[256,2048]{0,1:T(8,128)(2,1)} async-done(((bf16[1024,2048]{0,1:T(8,128)(2,1)}), bf16[256,2048]{0,1:T(8,128)(2,1)}) %reduce-scatter.26.cloned.1.call-update) | async-done | bytes 1048592 | tf_op jit(solution)/shard_map/reduce_scatter | solution.py:277
  718.3 74.2 %reduce-scatter.32.cloned.1.call-done = bf16[1024,1024]{1,0:T(8,128)(2,1)} async-done(((bf16[4096,1024]{1,0:T(8,128)(2,1)}), bf16[1024,1024]{1,0:T(8,128)(2,1)}) %reduce-scatter.32.cloned.1.call-update) | async-done | bytes 2097168 | tf_op jit(solution)/shard_map/reduce_scatter | solution.py:286
  792.5 74.4 %reduce-scatter.30.cloned.1.call-done = bf16[256,4096]{1,0:T(8,128)(2,1)} async-done(((bf16[1024,4096]{1,0:T(8,128)(2,1)}), bf16[256,4096]{1,0:T(8,128)(2,1)}) %reduce-scatter.30.cloned.1.call-update) | async-done | bytes 2097168 | tf_op jit(solution)/shard_map/reduce_scatter | solution.py:283
  866.9 60.8 %reduce-scatter.20.cloned.1.call-done = bf16[256,3072]{0,1:T(8,128)(2,1)} async-done(((bf16[1024,3072]{0,1:T(8,128)(2,1)}), bf16[256,3072]{0,1:T(8,128)(2,1)}) %reduce-scatter.20.cloned.1.call-update) | async-done | bytes 1572880 | tf_op jit(solution)/shard_map/reduce_scatter | solution.py:268
  927.7 23.2 %reduce-scatter.36.cloned.1.call-done = bf16[256,3]{1,0:T(8,128)(2,1)} async-done(((bf16[1024,3]{1,0:T(8,128)(2,1)}), bf16[256,3]{1,0:T(8,128)(2,1)}) %reduce-scatter.36.cloned.1.call-update) | async-done | bytes 1552
  951.8 22.0 %reduce-scatter.38.cloned.1.call-done = bf16[256,3]{1,0:T(8,128)(2,1)} async-done(((bf16[1024,3]{1,0:T(8,128)(2,1)}), bf16[256,3]{1,0:T(8,128)(2,1)}) %reduce-scatter.38.cloned.1.call-update) | async-done | bytes 1552
  974.7 22.3 %all-reduce = (bf16[3,256]{1,0:T(4,128)(2,1)S(1)}, bf16[3,256]{1,0:T(4,128)(2,1)S(1)}) all-reduce(bf16[3,256]{1,0:T(4,128)(2,1)S(1)} %copy.122, bf16[3,256]{1,0:T(4,128)(2,1)S(1)} %copy.124), channel_id=1, replica_groups=mesh['seq'=2,'ctx'=4,'fsdp'=4] {'seq','ctx'}, use_global_device_ids=true, to_apply=%region_42.43 | all-reduce | flops 1536 | bytes 6144 | tf_op jit(solution)/shard_map/psum | solution.py:304
  1008.5 246.6 %all-reduce.4.cloned.1.call-done = (bf16[256,3072]{0,1:T(8,128)(2,1)}, bf16[256,2048]{0,1:T(8,128)(2,1)}, bf16[256,1024]{1,0:T(8,128)(2,1)}, bf16[256,1024]{1,0:...) async-done(((bf16[256,3072]{0,1:T(8,128)(2,1)}, bf16[256,2048]{0,1:T(8,128)(2,1)}, bf16[256,1024]{1,0:T(8,128)(2,1)}, ...) | async-done | bytes 8388624 | tf_op jit(solution)/shard_map/psum | solution.py:297
  (298 shorter events, 241.6 us)
Async XLA Ops:
  7.2 39.6 %all-gather.17.cloned.1.call-start = ((), (), s32[]{:S(2)}) async-start(), calls=%async_computation.14 | async-start | bytes 5242880 | tf_op jit(solution)/shard_map/all_gather | solution.py:172
  7.9 86.9 %all-gather.11.cloned.1.call-start = ((), (), s32[]{:S(2)}) async-start(), calls=%async_computation.11 | async-start | bytes 7864320 | tf_op jit(solution)/shard_map/all_gather | solution.py:169
  8.7 116.2 %all-gather.27.cloned.1.call-start = ((), (), s32[]{:S(2)}) async-start(), calls=%async_computation.27 | async-start | bytes 1310720 | tf_op jit(solution)/shard_map/all_gather | solution.py:201
  50.6 156.6 %all-gather.13.cloned.1.call-start = ((), (), s32[]{:S(2)}) async-start(), calls=%async_computation.12 | async-start | bytes 5242880 | tf_op jit(solution)/shard_map/all_gather | solution.py:192
  101.6 153.0 %all-gather.15.cloned.1.call-start = ((), (), s32[]{:S(2)}) async-start(), calls=%async_computation.13 | async-start | bytes 2621440 | tf_op jit(solution)/shard_map/all_gather | solution.py:170
  102.2 155.4 %all-gather.19.cloned.1.call-start = ((), (), s32[]{:S(2)}) async-start(), calls=%async_computation.15 | async-start | bytes 2621440 | tf_op jit(solution)/shard_map/all_gather | solution.py:171
  102.8 175.2 %all-gather.21.cloned.1.call-start = ((), (), s32[]{:S(2)}) async-start(), calls=%async_computation.16 | async-start | bytes 2621440 | tf_op jit(solution)/shard_map/all_gather | solution.py:173
  103.5 234.4 %all-gather.23.cloned.1.call-start = ((), (), s32[]{:S(2)}) async-start(), calls=%async_computation.17 | async-start | bytes 10485760 | tf_op jit(solution)/shard_map/all_gather | solution.py:174
  104.3 293.5 %all-gather.25.cloned.1.call-start = ((), (), s32[]{:S(2)}) async-start(), calls=%async_computation.18 | async-start | bytes 10485760 | tf_op jit(solution)/shard_map/all_gather | solution.py:175
  105.0 395.3 %reduce-scatter.34.cloned.1.call-start = ((), (), s32[]{:S(2)}) async-start(), calls=%async_computation.28 | async-start | bytes 1310720
  116.1 162.0 %copy-start.39 = (f32[1,1024]{1,0:T(1,128)}, f32[1,1024]{1,0:T(1,128)S(1)}, u32[]{:S(2)}) copy-start(f32[1,1024]{1,0:T(1,128)S(1)} %get-tuple-element.523) | copy-start | bytes 12292
  127.4 138.1 %copy-start.10 = (bf16[1,256,1024]{1,2,0:T(8,128)(2,1)}, bf16[1,256,1024]{1,2,0:T(8,128)(2,1)S(1)}, u32[]{:S(2)}) copy-start(bf16[1,256,1024]{1,2,0:T(8,128)(2,1)S(1)} %copy.80) | copy-start | bytes 1572868
  280.6 144.4 %copy-start.5 = (f32[256,1024]{1,0:T(8,128)}, f32[256,1024]{1,0:T(8,128)S(1)}, u32[]{:S(2)}) copy-start(f32[256,1024]{1,0:T(8,128)S(1)} %get-tuple-element.531) | copy-start | bytes 3145732
  450.3 117.3 %reduce-scatter.18.cloned.1.call-start = ((), (), s32[]{:S(2)}) async-start(), calls=%async_computation.19 | async-start | bytes 5242880 | tf_op jit(solution)/shard_map/reduce_scatter | solution.py:257
  490.8 111.3 %reduce-scatter.28.cloned.1.call-start = ((), (), s32[]{:S(2)}) async-start(), calls=%async_computation.24 | async-start | bytes 2621440 | tf_op jit(solution)/shard_map/reduce_scatter | solution.py:280
  494.2 142.0 %reduce-scatter.24.cloned.1.call-start = ((), (), s32[]{:S(2)}) async-start(), calls=%async_computation.22 | async-start | bytes 2621440 | tf_op jit(solution)/shard_map/reduce_scatter | solution.py:274
  496.5 174.1 %reduce-scatter.22.cloned.1.call-start = ((), (), s32[]{:S(2)}) async-start(), calls=%async_computation.21 | async-start | bytes 2621440 | tf_op jit(solution)/shard_map/reduce_scatter | solution.py:271
  500.2 218.1 %reduce-scatter.26.cloned.1.call-start = ((), (), s32[]{:S(2)}) async-start(), calls=%async_computation.23 | async-start | bytes 5242880 | tf_op jit(solution)/shard_map/reduce_scatter | solution.py:277
  505.4 287.1 %reduce-scatter.32.cloned.1.call-start = ((), (), s32[]{:S(2)}) async-start(), calls=%async_computation.26 | async-start | bytes 10485760 | tf_op jit(solution)/shard_map/reduce_scatter | solution.py:286
  513.9 353.0 %reduce-scatter.30.cloned.1.call-start = ((), (), s32[]{:S(2)}) async-start(), calls=%async_computation.25 | async-start | bytes 10485760 | tf_op jit(solution)/shard_map/reduce_scatter | solution.py:283
  522.5 405.2 %reduce-scatter.20.cloned.1.call-start = ((), (), s32[]{:S(2)}) async-start(), calls=%async_computation.20 | async-start | bytes 7864320 | tf_op jit(solution)/shard_map/reduce_scatter | solution.py:268
  573.4 377.4 %reduce-scatter.36.cloned.1.call-start = ((), (), s32[]{:S(2)}) async-start(), calls=%async_computation.29 | async-start | bytes 327680
  575.5 398.3 %reduce-scatter.38.cloned.1.call-start = ((), (), s32[]{:S(2)}) async-start(), calls=%async_computation.30 | async-start | bytes 327680
  576.5 678.6 %all-reduce.4.cloned.1.call-start = ((), (), s32[]{:S(2)}) async-start(), calls=%async_computation.31 | async-start | bytes 16777216 | tf_op jit(solution)/shard_map/psum | solution.py:297
  (44 other events, 396.6 us)
Sparse Core Ops, SparseCore 0:
  9.6 37.1 all-gather.16
  48.4 46.3 all-gather.10
  96.9 27.9 all-gather.26
  126.9 80.2 all-gather.12
  208.6 21.1 all-gather.14
  231.2 22.6 all-gather.18
  255.4 22.5 all-gather.20
  279.6 58.2 all-gather.22
  339.5 58.2 all-gather.24
  450.5 27.1 reduce-scatter.33
  490.9 76.7 reduce-scatter.17
  570.1 31.9 reduce-scatter.27
  604.7 31.4 reduce-scatter.23
  639.2 31.4 reduce-scatter.21
  673.8 44.5 reduce-scatter.25
  720.7 71.6 reduce-scatter.31
  795.1 71.7 reduce-scatter.29
  869.2 58.3 reduce-scatter.19
  930.8 19.9 reduce-scatter.35
  953.7 20.0 reduce-scatter.37
  980.2 274.8 all-reduce.3
where the time goes:
time: 1280 us
  waiting for transfers between devices  971 us (76%)
  matrix products  156 us (12%)
  local copies, waits for them, and re-layouts  61.5 us (5%)
  other arithmetic  34.7 us (3%)
  blocking collectives  32.9 us (3%)
  between operations  15.6 us (1%)
    psum x1, waiting for transfers between devices, local(): lax.psum(shards[0].astype(jnp.bfloat16), ('seq', 'ctx')).astype(jnp.float32)  247 us
    all_gather x1, waiting for transfers between devices, local(): keys_all = lax.all_gather(keyval, 'ctx', axis=1, tiled=True)  78.3 us
    reduce_scatter x1, waiting for transfers between devices, local(): lax.psum_scatter(grad_ff_in.astype(jnp.bfloat16), 'fsdp', scatter_dimensi...  74.4 us
    reduce_scatter x1, waiting for transfers between devices, local(): lax.psum_scatter(grad_ff_out.astype(jnp.bfloat16), 'fsdp', scatter_dimens...  74.2 us
    reduce_scatter x1, waiting for transfers between devices, local(): lax.psum_scatter(grad_attn_qkv.astype(jnp.bfloat16), 'fsdp', scatter_dime...  60.8 us
    all_gather x1, waiting for transfers between devices, local(): lax.all_gather(ff_in, 'fsdp', axis=0, tiled=True)  57 us
    unnamed x24, waiting for transfers between devices  50 us
    reduce_scatter x1, waiting for transfers between devices, local(): lax.psum_scatter(grad_cross_kv.astype(jnp.bfloat16), 'fsdp', scatter_dime...  47.7 us
  transfers between devices with their start and end apart: 21, of which 18 were waited for; matrix products, arithmetic and copies ran while one was open for 14% of the time, Pallas kernels for 0%

commit v1 on v0

v1 whole, which is shorter than its diff:
```python
import functools

import jax
import jax.numpy as jnp
from jax import lax
from jax.experimental import pallas as pl
from jax.experimental.pallas import tpu as pltpu
from jax.sharding import PartitionSpec as P

HEADS = 16
HEAD_DIM = 64
TILE = 256
GROUP = 4
VMEM_LIMIT = 48 * 1024 * 1024
BF = jnp.bfloat16
F32 = jnp.float32
SMEM = pl.BlockSpec(memory_space=pltpu.SMEM)


def dot(left, right):
    return jnp.dot(left, right, preferred_element_type=F32)


def dot_rows(left, right):
    return lax.dot_general(left, right, (((0,), (0,)), ((), ())), preferred_element_type=F32)


def dot_cols(left, right):
    return lax.dot_general(left, right, (((1,), (1,)), ((), ())), preferred_element_type=F32)


def after(value, *others):
    return lax.optimization_barrier((value, *others))[0]


def causal_mask(tile):
    key = lax.broadcasted_iota(jnp.int32, (tile, tile), 0)
    query = lax.broadcasted_iota(jnp.int32, (tile, tile), 1)
    return key <= query


def lanes_of(heads):
    return [slice(head * HEAD_DIM, (head + 1) * HEAD_DIM) for head in range(heads)]


def joined_heads(values, axis):
    return values[0] if len(values) == 1 else jnp.concatenate(values, axis)


def spans(causal, at, keys):
    if not causal:
        return [(0, keys, False)]
    return ([(0, at * TILE, False)] if at else []) + [(at * TILE, TILE, True)]


def attend_kernel(causal, heads, steps, q_ref, k_ref, v_ref, out_ref, out_t_ref, lse_ref):
    query = q_ref[...] * HEAD_DIM**-0.5
    lanes = lanes_of(heads)

    def finish(outs):
        out_t = joined_heads(outs, 0)
        out_t_ref[...] = out_t
        out_ref[...] = out_t.T.astype(BF)

    def whole(at):
        parts = spans(causal, at, k_ref.shape[0])
        outs = []
        for head, lane in enumerate(lanes):
            scores = []
            for start, size, masked in parts:
                score = dot_cols(k_ref[start : start + size, lane], query[:, lane])
                scores.append(jnp.where(causal_mask(TILE), score, -1e30) if masked else score)
            top = functools.reduce(jnp.maximum, [jnp.max(score, 0, keepdims=True) for score in scores])
            probs = [jnp.exp(score - top) for score in scores]
            total = sum(jnp.sum(prob, 0, keepdims=True) for prob in probs)
            accum = sum(
                dot_rows(v_ref[start : start + size, lane], prob.astype(BF))
                for (start, size, _), prob in zip(parts, probs)
            )
            outs.append(accum / total)
            lse_ref[head : head + 1, :] = top + jnp.log(total)
        finish(outs)

    def rolled(at):
        def step(index, carry, masked):
            span = pl.ds(pl.multiple_of(index * TILE, TILE), TILE)
            keys, values = k_ref[span, :], v_ref[span, :]
            after_step = []
            for head, lane in enumerate(lanes):
                top, total, accum = carry[head]
                score = dot_cols(keys[:, lane], query[:, lane])
                if masked:
                    score = jnp.where(causal_mask(TILE), score, -1e30)
                new_top = jnp.maximum(top, jnp.max(score, 0, keepdims=True))
                prob = jnp.exp(score - new_top)
                decay = jnp.exp(top - new_top)
                total = total * decay + jnp.sum(prob, 0, keepdims=True)
                accum = accum * decay + dot_rows(values[:, lane], prob.astype(BF))
                after_step.append((new_top, total, accum))
            return tuple(after_step)

        rows = query.shape[0]
        carry = tuple(
            (
                jnp.full((1, rows), -1e30, F32),
                jnp.zeros((1, rows), F32),
                jnp.zeros((HEAD_DIM, rows), F32),
            )
            for _ in lanes
        )
        carry = lax.fori_loop(0, at, functools.partial(step, masked=False), carry)
        carry = step(at, carry, True)
        for head in range(heads):
            lse_ref[head : head + 1, :] = carry[head][0] + jnp.log(carry[head][1])
        finish([accum / total for _, total, accum in carry])

    run_tiles(causal, steps, whole, rolled)


def run_tiles(causal, steps, whole, rolled):
    at = pl.program_id(1)
    if not causal:
        whole(0)
    elif steps <= 4:
        for tile in range(steps):
            pl.when(at == tile)(functools.partial(whole, tile))
    else:
        rolled(at)


def attend_back_kernel(
    causal, heads, steps, q_ref, k_ref, v_ref, do_ref, out_t_ref, lse_ref,
    dq_ref, dk_ref, dv_ref, dk_sum, dv_sum,
):
    query = q_ref[...] * HEAD_DIM**-0.5
    d_out = do_ref[...]
    lanes = lanes_of(heads)
    weighed = d_out.astype(F32).T * out_t_ref[...]
    deltas = [jnp.sum(weighed[lane, :], 0, keepdims=True) for lane in lanes]
    totals = [lse_ref[head : head + 1, :] for head in range(heads)]

    @pl.when(pl.program_id(1) == 0)
    def _():
        dk_sum[...] = jnp.zeros_like(dk_sum)
        dv_sum[...] = jnp.zeros_like(dv_sum)

    def part(span, masked, d_query):
        keys, values = k_ref[span, :], v_ref[span, :]
        d_keys, d_values, out = [], [], []
        for head, lane in enumerate(lanes):
            score = dot_cols(keys[:, lane], query[:, lane])
            prob = jnp.exp(score - totals[head])
            if masked:
                prob = jnp.where(causal_mask(TILE), prob, 0.0)
            d_prob = dot_cols(values[:, lane], d_out[:, lane])
            d_score = (prob * (d_prob - deltas[head])).astype(BF)
            d_values.append(dot(prob.astype(BF), d_out[:, lane]))
            d_keys.append(dot(d_score, query[:, lane]))
            out.append(d_query[head] + dot_rows(keys[:, lane], d_score))
        dk_sum[span, :] += joined_heads(d_keys, 1)
        dv_sum[span, :] += joined_heads(d_values, 1)
        return tuple(out)

    start = tuple(jnp.zeros((HEAD_DIM, query.shape[0]), F32) for _ in lanes)

    def finish(d_query):
        dq_ref[...] = (joined_heads(d_query, 0).T * HEAD_DIM**-0.5).astype(BF)

    def whole(at):
        d_query = start
        for first, size, masked in spans(causal, at, k_ref.shape[0]):
            d_query = part(slice(first, first + size), masked, d_query)
        finish(d_query)

    def rolled(at):
        def step(index, carry):
            return part(pl.ds(pl.multiple_of(index * TILE, TILE), TILE), False, carry)

        d_query = lax.fori_loop(0, at, step, start)
        finish(part(pl.ds(pl.multiple_of(at * TILE, TILE), TILE), True, d_query))

    run_tiles(causal, steps, whole, rolled)

    @pl.when(pl.program_id(1) == steps - 1)
    def _():
        dk_ref[...] = dk_sum[...].astype(BF)
        dv_ref[...] = dv_sum[...].astype(BF)


def attend_specs(rows, keys, width, parts):
    group = min(width, GROUP * HEAD_DIM)
    groups = width // group

    def tall(part):
        return pl.BlockSpec((keys, group), lambda g, i: (0, part * groups + g))

    def query(part):
        return pl.BlockSpec((TILE, group), lambda g, i: (i, part * groups + g))

    return (
        (groups, rows // TILE), group, query(0), tall(parts[0]), tall(parts[1]), tall(0),
        pl.BlockSpec((group, TILE), lambda g, i: (g, i)),
        pl.BlockSpec((8, TILE), lambda g, i: (g, i)),
    )


def attend(causal, query, keys, values, width, parts):
    rows, depth = query.shape[0], keys.shape[0]
    grid, group, q_spec, k_spec, v_spec, _, t_spec, lse_spec = attend_specs(rows, depth, width, parts)
    return pl.pallas_call(
        functools.partial(attend_kernel, causal, group // HEAD_DIM, grid[1]),
        grid=grid,
        in_specs=[q_spec, k_spec, v_spec],
        out_specs=[q_spec, t_spec, lse_spec],
        out_shape=[
            jax.ShapeDtypeStruct((rows, width), BF),
            jax.ShapeDtypeStruct((width, rows), F32),
            jax.ShapeDtypeStruct((8 * grid[0], rows), F32),
        ],
        compiler_params=pltpu.CompilerParams(vmem_limit_bytes=VMEM_LIMIT),
        cost_estimate=pl.CostEstimate(
            flops=4 * rows * depth * width, bytes_accessed=8 * (rows + depth) * width,
            transcendentals=rows * depth * width // HEAD_DIM,
        ),
    )(query, keys, values)


def attend_back(causal, query, keys, values, d_out, out_t, lse, width, parts):
    rows, depth = query.shape[0], keys.shape[0]
    grid, group, q_spec, k_spec, v_spec, tall, t_spec, lse_spec = attend_specs(rows, depth, width, parts)
    return pl.pallas_call(
        functools.partial(attend_back_kernel, causal, group // HEAD_DIM, grid[1]),
        grid=grid,
        in_specs=[q_spec, k_spec, v_spec, q_spec, t_spec, lse_spec],
        out_specs=[q_spec, tall, tall],
        out_shape=[
            jax.ShapeDtypeStruct((rows, width), BF),
            jax.ShapeDtypeStruct((depth, width), BF),
            jax.ShapeDtypeStruct((depth, width), BF),
        ],
        scratch_shapes=[pltpu.VMEM((depth, group), F32), pltpu.VMEM((depth, group), F32)],
        compiler_params=pltpu.CompilerParams(vmem_limit_bytes=VMEM_LIMIT),
        cost_estimate=pl.CostEstimate(
            flops=10 * rows * depth * width, bytes_accessed=12 * (rows + depth) * width,
            transcendentals=rows * depth * width // HEAD_DIM,
        ),
    )(query, keys, values, d_out, out_t, lse)


IN_VMEM = pl.BlockSpec(memory_space=pltpu.VMEM)


def moved(kernel, scalars, values, out_shapes, dtype=BF):
    size = sum(value.size * value.dtype.itemsize for value in values)
    return pl.pallas_call(
        kernel,
        in_specs=[SMEM] * len(scalars) + [IN_VMEM] * len(values),
        out_specs=[IN_VMEM] * len(out_shapes),
        out_shape=[jax.ShapeDtypeStruct(shape, dtype) for shape in out_shapes],
        compiler_params=pltpu.CompilerParams(vmem_limit_bytes=VMEM_LIMIT),
        cost_estimate=pl.CostEstimate(flops=0, bytes_accessed=2 * size, transcendentals=0),
    )(*scalars, *values)


def place(rows, pieces, starts, *scalars):
    def kernel(*refs):
        values, out_ref = refs[len(scalars) : -1], refs[-1]
        for start, value in zip(starts(*refs[: len(scalars)]), values):
            out_ref[pl.ds(pl.multiple_of(start, 16), value.shape[0]), :] = value[...]

    return moved(kernel, scalars, pieces, [(rows, pieces[0].shape[1])])[0]


def cut(value, rows, count, starts, *scalars):
    def kernel(*refs):
        source, outs = refs[len(scalars)], refs[len(scalars) + 1 :]
        first = starts(*refs[: len(scalars)])
        size = rows // 2
        for index, start in enumerate(first):
            outs[index // 2][index % 2 * size : (index % 2 + 1) * size, :] = source[
                pl.ds(pl.multiple_of(start, 16), size), :
            ]

    return moved(kernel, scalars, [value], [(rows, value.shape[1])] * count)


def line_up(pieces, parts, at, dtype=BF):
    rows, columns = pieces[0].shape
    size = columns // parts

    def kernel(at_ref, *refs):
        values, out_ref = refs[:-1], refs[-1]
        for mask, value in enumerate(values):
            owner = at_ref[0] ^ mask
            for part in range(parts):
                start = part * size * len(values) + owner * size
                out_ref[:, pl.ds(pl.multiple_of(start, 128), size)] = value[
                    :, part * size : (part + 1) * size
                ].astype(dtype)

    return moved(kernel, [at], pieces, [(rows, columns * len(pieces))], dtype)[0]


def turn(value, starts, *scalars):
    def kernel(*refs):
        source, out_ref = refs[len(scalars) :]
        first = starts(*refs[: len(scalars)])
        size = source.shape[1] // len(first)
        for index, start in enumerate(first):
            out_ref[:, index * size : (index + 1) * size] = source[
                :, pl.ds(pl.multiple_of(start, 128), size)
            ]

    return moved(kernel, scalars, [value], [value.shape])[0]


def two_halves(kernel, own, other, at, out_widths):
    rows = out_widths[0][0]

    def body(at_ref, own_ref, other_ref, *outs):
        here = pl.program_id(0) == at_ref[0]
        pl.when(here)(lambda: kernel(own_ref, *outs))
        pl.when(jnp.logical_not(here))(lambda: kernel(other_ref, *outs))

    whole = pl.BlockSpec(own.shape, lambda i: (0, 0))
    return pl.pallas_call(
        body,
        grid=(2,),
        in_specs=[SMEM, whole, whole],
        out_specs=[pl.BlockSpec((rows, width), lambda i: (i, 0)) for _, width in out_widths],
        out_shape=[jax.ShapeDtypeStruct((2 * rows, width), F32) for _, width in out_widths],
        compiler_params=pltpu.CompilerParams(vmem_limit_bytes=VMEM_LIMIT),
        cost_estimate=pl.CostEstimate(flops=0, bytes_accessed=12 * own.size, transcendentals=0),
    )(at, own, other)


def split_columns_kernel(widths, source, *outs):
    at = 0
    for width, out in zip(widths, outs):
        out[...] = source[:, at : at + width].astype(F32)
        at += width


def spread_parts_kernel(owners, parts, source, out):
    rows, size = out.shape[0], source.shape[1] // parts
    width = out.shape[1] // parts
    for owner in range(owners):
        for part in range(parts):
            out[:, part * width + owner * size : part * width + (owner + 1) * size] = source[
                owner * rows : (owner + 1) * rows, part * size : (part + 1) * size
            ].astype(F32)


def norm_parts(value):
    centre = jnp.mean(value, -1, keepdims=True)
    centred = value - centre
    spread = jnp.mean(centred * centred, -1, keepdims=True)
    scale = lax.rsqrt(spread + 1e-05)
    return centred * scale, scale


def norm_back(grad, unit, scale, gain):
    slope = grad * gain
    d_value = scale * (
        slope
        - jnp.mean(slope, -1, keepdims=True)
        - unit * jnp.mean(slope * unit, -1, keepdims=True)
    )
    return d_value, jnp.sum(grad * unit, 0, keepdims=True), jnp.sum(grad, 0, keepdims=True)


def local(
    S, C, F,
    hidden, encoder, attn_qkv, attn_out, cross_q, cross_kv, cross_out, ff_in, ff_out,
    norm_gains, norm_biases, block_table, out_grad,
):
    rows, width = hidden.shape[1:]
    enc_rows = encoder.shape[1]
    half = rows // 2
    K = 2
    Y = F // K
    head_width = width // C
    ff_width = ff_in.shape[1] // F
    s, c, f = (lax.axis_index(name).astype(jnp.uint32) for name in ("seq", "ctx", "fsdp"))
    index_of = {"seq": s, "ctx": c, "fsdp": f}
    size_of = {"seq": S, "ctx": C, "fsdp": F}
    s_scalar, c_scalar, f_scalar = (index.astype(jnp.int32).reshape(1) for index in (s, c, f))

    def pick(value, index, axis=0):
        return lax.dynamic_index_in_dim(value, index, axis, keepdims=False)

    def bits_of(axis):
        return [1 << i for i in range(size_of[axis].bit_length() - 1)]

    def swap(value, axis, mask):
        return lax.ppermute(value, axis, [(i, i ^ mask) for i in range(size_of[axis])])

    def is_low(axis, bit):
        return (index_of[axis] & bit) == 0

    def give(parts, axis, bit):
        view = parts.reshape(parts.shape[0] // 2, 2, *parts.shape[1:])
        mine = (index_of[axis] // bit) & 1
        return pick(view, mine, 1), swap(pick(view, mine ^ 1, 1), axis, bit)

    def double(value, got, axis, bit):
        both = jnp.where(
            is_low(axis, bit), jnp.stack([value, got], 1), jnp.stack([got, value], 1)
        )
        return both.reshape(2 * value.shape[0], *value.shape[1:])

    def gather_over(value, axis):
        value = value[None]
        for bit in reversed(bits_of(axis)):
            value = double(value, swap(value, axis, bit), axis, bit)
        return value

    def by_owner_of(got, axis):
        stacked = jnp.stack(got)
        for bit in bits_of(axis):
            view = stacked.reshape(size_of[axis] // (2 * bit), 2, bit, *stacked.shape[1:])
            view = jnp.where(is_low(axis, bit), view, view[:, ::-1])
            stacked = view.reshape(stacked.shape)
        return stacked

    def exchanged(piece_of, axis):
        index = index_of[axis]
        return [piece_of(index)] + [
            swap(piece_of(index ^ mask), axis, mask) for mask in range(1, size_of[axis])
        ]

    def my_columns(weight, parts):
        size = weight.shape[1] // parts
        return jnp.concatenate(
            [
                lax.dynamic_slice_in_dim(weight, part * size + c * head_width, head_width, 1)
                for part in range(parts)
            ],
            1,
        )

    def to_rows(value):
        def starts(c_ref, table_ref):
            return [table_ref[c_ref[0] ^ mask, b] * half for mask in range(C) for b in range(2)]

        pieces = cut(value, rows, C, starts, c_scalar, block_table)
        return [pieces[0]] + [swap(pieces[mask], "ctx", mask) for mask in range(1, C)]

    def columns_in_order(got, parts):
        size = got[0].shape[1] // parts
        if size % 128 == 0:
            return line_up(got, parts, c_scalar)
        view = by_owner_of(got, "ctx").reshape(C, got[0].shape[0], parts, size)
        return view.transpose(1, 2, 0, 3).reshape(got[0].shape[0], C * parts * size)

    def to_columns(got):
        pieces = [value[b * half : (b + 1) * half] for value in got for b in range(2)]

        def starts(c_ref, table_ref):
            return [table_ref[c_ref[0] ^ mask, b] * half for mask in range(C) for b in range(2)]

        return place(C * rows, pieces, starts, c_scalar, block_table)

    def joined(lefts, rights):
        return dot_rows(jnp.concatenate(lefts, 0), jnp.concatenate(rights, 0)).astype(BF)

    flat = hidden.reshape(rows, width)
    enc = encoder.reshape(enc_rows, width)
    near = list(range(1, K))
    far = [mask for mask in range(F) if mask >= K]

    def near_first(size):
        return lambda f_ref: [(f_ref[0] ^ mask) * size for mask in range(F)]

    def spread(value):
        got = {mask: swap(value, "fsdp", mask) for mask in near}
        got.update({mask: swap(value, "fsdp", mask) for mask in far if mask % K == 0})
        return got

    def passed_on(got):
        return {mask: swap(got[mask - mask % K], "fsdp", mask % K) for mask in far if mask % K}

    slice_here = my_columns(attn_qkv, 3)
    norms = jnp.concatenate([norm_gains, norm_biases], 0)
    x_moving = [flat[:half], flat[half:]]
    x_pieces = list(x_moving)
    seen = []
    for step in range(C - 1):
        sent = {"x": [lax.ppermute(v, "ctx", [(i, (i + 1) % C) for i in range(C)]) for v in x_moving]}
        if step == 0:
            sent["slices"] = spread(slice_here)
            sent["norms"] = swap(norms, "fsdp", F // 2)
        sent = lax.optimization_barrier(sent)
        x_moving = sent["x"]
        x_pieces += x_moving
        seen.append(x_moving[0])
        if step == 0:
            slices, norms_got = sent["slices"], sent["norms"]
            slices.update(passed_on(slices))
            norms = double(norms[None], norms_got[None], "fsdp", F // 2)
            for bit in reversed(bits_of("fsdp")[:-1]):
                norms = double(norms, swap(norms, "fsdp", bit), "fsdp", bit)
    outs = spread(after(attn_out, seen[0]))
    outs.update(passed_on(outs))
    size = attn_qkv.shape[0]
    w_mine = place(width, [slice_here] + [slices[mask] for mask in near + far], near_first(size), f_scalar)
    w_out = place(width, [attn_out] + [outs[mask] for mask in near + far], near_first(size), f_scalar)
    norms = norms.astype(F32).transpose(1, 0, 2).reshape(6, width)
    gains, shifts = norms[:3], norms[3:]

    def x_starts(c_ref, table_ref):
        return [table_ref[(c_ref[0] + C - hop) & (C - 1), b] * half for hop in range(C) for b in range(2)]

    x_all = place(C * rows, x_pieces, x_starts, c_scalar, block_table)

    def gather(shard):
        return lax.all_gather(shard, "fsdp", axis=0, tiled=True)

    w_ckv = gather(cross_kv)
    w_cq, w_co = gather(after(cross_q, seen[0])), gather(after(cross_out, seen[0]))
    ff_later = after(ff_in, x_moving[0])
    ff_pieces = exchanged(
        lambda owner: lax.dynamic_slice_in_dim(ff_later, owner * ff_width, ff_width, 1), "fsdp"
    )
    w_ff = ff_out

    turns = [0]
    for bit in reversed(bits_of("fsdp")):
        turns = turns + [turn | bit for turn in turns]

    def turned(value):
        size = value.shape[1] // (F * S)
        if size % 128 == 0:
            return turn(
                value,
                lambda f_ref, s_ref: [
                    (f_ref[0] ^ mask) * (S * size) + (s_ref[0] ^ there) * size
                    for mask in turns
                    for there in range(S)
                ],
                f_scalar,
                s_scalar,
            )
        blocks = []
        for mask in turns:
            for there in range(S):
                at = (f ^ mask) * (S * size) + (s ^ there) * size
                blocks.append(lax.dynamic_slice_in_dim(value, at, size, 1))
        return jnp.concatenate(blocks, 1)

    class Tall:
        levels = [("fsdp", bit) for bit in bits_of("fsdp")] + [("seq", bit) for bit in bits_of("seq")]

        def __init__(self, left, right):
            self.left, self.right, self.got = left, right, []
            self.size = left.shape[1]
            self.at = 0

        def term(self, start, stop, token):
            right, got = self.right, self.got
            if token is not None:
                right, got = lax.optimization_barrier((right, got, token))[:2]
            total = dot_rows(self.left[:, start:stop], right)
            for value in got:
                total = total + value[start:stop].astype(F32)
            return total.astype(BF)

        def start(self, token=None, count=1):
            for _ in range(count):
                axis, bit = self.levels[self.at]
                self.at += 1
                self.size //= 2
                sent = self.term(self.size, 2 * self.size, token)
                self.got.append(swap(sent, axis, bit))
            return sent

        def end(self, token=None):
            return self.term(0, self.size, token)

    enc_all = after(enc, x_moving[0])[None]
    for bit in reversed(bits_of("ctx")):
        enc_some, enc_all = enc_all, double(enc_all, swap(enc_all, "ctx", bit), "ctx", bit)
    enc_all = enc_all.reshape(C * enc_rows, width)
    qkv = after(dot(x_all, w_mine).astype(BF), enc_some)
    if head_width % (2 * HEAD_DIM) == 0:
        self_in, self_parts = (qkv, qkv, qkv), (1, 2)
    else:
        self_in, self_parts = jnp.split(qkv, 3, 1), (0, 0)
    att_mine, att_t, att_lse = attend(True, *self_in, head_width, self_parts)
    att = columns_in_order(to_rows(att_mine), 1)
    ekv = dot(enc_all, w_ckv).astype(BF)
    w_in = place(width, ff_pieces, near_first(size), f_scalar)
    unit_0, scale_0 = norm_parts(flat.astype(F32) + dot(att, w_out))
    h_1 = unit_0 * gains[0] + shifts[0]
    h_1_low = h_1.astype(BF)

    cq = dot(h_1_low, w_cq).astype(BF)
    cat, cat_t, cat_lse = attend(False, cq, ekv, ekv, width, (0, 1))
    unit_1, scale_1 = norm_parts(h_1 + dot(cat, w_co))
    h_2 = unit_1 * gains[1] + shifts[1]
    h_2_low = h_2.astype(BF)

    def exchange(value, work, close):
        moving = {dy: swap(value, "fsdp", dy * K) for dy in range(1, Y)}

        def with_pair(there):
            return jnp.concatenate([there] + [swap(there, "fsdp", mask) for mask in near], 0)

        def pair_sum(term):
            view = term.astype(BF).reshape(K, -1, term.shape[1])
            total = view[0].astype(F32)
            for mask in near:
                total = total + swap(view[mask], "fsdp", mask).astype(F32)
            return total

        group = [with_pair(value)]
        worked = [work(0, group[0])]
        last = worked[0][0]
        for dy in range(1, Y):
            group.append(with_pair(after(moving[dy], last)))
            worked.append(work(dy, group[dy]))
            last = worked[dy][0]
        back, sent = [], None
        for dy in range(1, Y):
            sent = pair_sum(close(worked[dy])).astype(BF)
            back.append(swap(sent, "fsdp", dy * K))

        def finish(hold=()):
            own = worked[0] if sent is None else lax.optimization_barrier((worked[0], sent))[0]
            own = pair_sum(close(own))
            got = lax.optimization_barrier((back, own, hold))[0] if back else back
            return sum((value.astype(F32) for value in got), own)

        return group, worked, sent if back else last, finish

    def feed_forward(dy, value):
        pre = dot(value, w_in)
        cdf = 0.5 * (1.0 + lax.erf(pre * 0.5**0.5))
        slope = cdf + pre * (jnp.exp(-0.5 * pre * pre) * (2.0 * jnp.pi) ** -0.5)
        return lax.optimization_barrier(((pre * cdf).astype(BF), slope))

    h_2_rows, worked, _, finish = exchange(h_2_low, feed_forward, lambda got: dot(got[0], w_ff))
    acts, slopes = [got[0] for got in worked], [got[1] for got in worked]
    x_later, enc_later, w_out_later = (after(value, h_2_low) for value in (x_all, enc_all, w_out))
    x_turned, enc_turned = turned(x_later), turned(enc_later)
    cat_turned, h_1_turned, att_turned = turned(cat), turned(h_1_low), turned(after(att, h_2_low))
    w_out_turned = w_out_later.reshape(C, head_width, width)
    w_out_turned = [pick(w_out_turned, c ^ mask) for mask in range(C)]
    total = finish((x_turned, enc_turned, cat_turned, h_1_turned, att_turned, w_out_turned))
    unit_2, scale_2 = norm_parts(h_2 + total)

    grad = out_grad.reshape(rows, width).astype(F32)
    d_r3, d_gain_2, d_shift_2 = norm_back(grad, unit_2, scale_2, gains[2])

    def feed_back(dy, value):
        return ((dot_cols(value, w_ff) * slopes[dy]).astype(BF),)

    df_rows, worked, sent, finish = exchange(
        d_r3.astype(BF), feed_back, lambda got: dot_cols(got[0], w_in)
    )
    d_pres = [got[0] for got in worked]

    def by_owner(partial):
        return partial.astype(BF).reshape(F, -1, partial.shape[1])

    first_of = {axis: bits_of(axis)[:1] for axis in size_of}
    rest_of = {axis: bits_of(axis)[1:] for axis in size_of}

    class Sum:
        def __init__(self, parts, dtype=BF):
            self.value, self.pair, self.dtype = parts, None, dtype

        def start(self, axis, bits, token, kind="halve"):
            for at, bit in enumerate(bits):
                if at:
                    self.end()
                value = after(self.value, token)
                self.pair = give(value, axis, bit) if kind == "halve" else (value, swap(value, axis, bit))
                self.how = (kind, axis, bit)

        def end(self, token=None):
            if self.pair is None:
                return
            kept, got = self.pair
            self.pair = None
            if token is not None:
                got = after(got, token)
            if self.how[0] == "double":
                self.value = double(kept, got, *self.how[1:])
            else:
                self.value = (kept.astype(F32) + got.astype(F32)).astype(self.dtype)

        def shape(self, *shape):
            self.value = self.value.reshape(*shape)

    ctx_up, ctx_last = rest_of["ctx"][::-1], first_of["ctx"]
    seq_bits = bits_of("seq")

    tile_ff_in = joined([after(value, sent) for value in h_2_rows], d_pres)
    tile_ff_out = joined([after(act, sent) for act in acts], df_rows)
    tile_ff_in, tile_ff_out = lax.optimization_barrier((tile_ff_in, tile_ff_out))
    def turned_chunks(value):
        split = [2] * (C.bit_length() - 1)
        view = value.reshape(S, *split, *value.shape[1:])
        axes = (0, *range(len(split), 0, -1), len(split) + 1, len(split) + 2)
        return view.transpose(*axes).reshape(value.shape)

    tiles = jnp.concatenate(
        [
            turned_chunks(tile_ff_out.reshape(S * C, -1, width)),
            turned_chunks(
                tile_ff_in.reshape(F, S * C, -1, ff_width).transpose(1, 0, 2, 3).reshape(S * C, -1, width)
            ),
        ],
        1,
    )
    tile_rows = tiles.shape[1]
    d_h2 = d_r3 + finish((tiles,))

    def pair_sum_over(value, axis, bit):
        groups = [[i, i | bit] for i in range(size_of[axis]) if not i & bit]
        return lax.psum_scatter(value, axis, scatter_dimension=0, axis_index_groups=groups, tiled=True)

    part = pair_sum_over(tiles.reshape(-1, width), "seq", 1)

    qkv_shards = spread(after(attn_qkv, d_h2))
    d_r2, d_gain_1, d_shift_1 = norm_back(d_h2, unit_1, scale_1, gains[1])
    dc = d_r2.astype(BF)
    d_cat = dot_cols(dc, w_co).astype(BF)
    co = Tall(cat_turned, dc)
    token = co.start(d_cat)
    dcq, dek, dev = attend_back(False, cq, ekv, ekv, after(d_cat, token), cat_t, cat_lse, width, (0, 1))

    d_h1 = d_r2 + dot_cols(dcq, w_cq)
    d_r1, d_gain_0, d_shift_0 = norm_back(d_h1, unit_0, scale_0, gains[0])
    da = d_r1.astype(BF)
    d_att_pieces = [dot_cols(da, piece).astype(BF) for piece in w_out_turned]

    d_att_got = [d_att_pieces[0]] + [swap(d_att_pieces[mask], "ctx", mask) for mask in range(1, C)]
    t3 = (d_att_pieces, d_att_got[1] if C > 1 else ())
    fsdp_rest = len(rest_of["fsdp"])
    norm_terms = jnp.concatenate([d_gain_0, d_gain_1, d_gain_2, d_shift_0, d_shift_1, d_shift_2], 0)
    norm_sum = Sum(norm_terms.reshape(6, F, width // F).transpose(1, 0, 2), F32)
    norm_sum.start("fsdp", first_of["fsdp"], t3)
    cq_, ck, cv, ao = (
        Tall(left, right)
        for left, right in ((h_1_turned, dcq), (enc_turned, dek), (enc_turned, dev), (att_turned, da))
    )
    token = t3
    for one in (cq_, ck, cv, ao):
        token = one.start(token)
    qkv_shards = after(qkv_shards, token)
    qkv_shards.update(passed_on(qkv_shards))
    norm_sum.end(token)
    norm_sum.start("fsdp", rest_of["fsdp"], token)
    for one in (co, cq_, ck, cv, ao):
        token = one.start(token, fsdp_rest)
    mixed = after((unit_2 * gains[2] + shifts[2]).astype(BF), token)
    enc_term = dot_cols(after(dek, token), w_ckv[:, :width]) + dot_cols(dev, w_ckv[:, width:])
    enc_term = enc_term.astype(BF)
    d_att = to_columns([after(value, token, enc_term, qkv_shards) for value in d_att_got])

    d_att, part = lax.optimization_barrier((d_att, part))
    part = pair_sum_over(part, "ctx", 1)
    dq, dk, dv = attend_back(True, *self_in, d_att, att_t, att_lse, head_width, self_parts)
    dqkv_mine = jnp.concatenate([dq, dk, dv], 1)

    t5 = dqkv_mine
    w_qkv = place(
        width,
        [attn_qkv] + [after(qkv_shards[mask], t5) for mask in near + far],
        near_first(attn_qkv.shape[0]),
        f_scalar,
    )
    qkv = Tall(x_turned, dqkv_mine)
    token = qkv.start(t5)
    norm_sum.end(t5)
    norm_sum.start("seq", seq_bits, t5, "swap")
    dqkv = to_rows(dqkv_mine)
    gots = (co.got, cq_.got, ck.got, cv.got, ao.got)
    dqkv, w_qkv, gots, part = lax.optimization_barrier((dqkv, w_qkv, gots, part))
    for bit in rest_of["ctx"]:
        part = pair_sum_over(part, "ctx", bit)
    whole = lax.all_gather(part, "ctx", axis=0, tiled=True)
    for one, got in zip((co, cq_, ck, cv, ao), gots):
        one.got = got
        token = one.start(token)
    token = qkv.start(token, fsdp_rest)
    norm_sum.end(token)
    five = [one.end(token) for one in (co, cq_, ck, cv, ao)]
    t6 = (five, norm_sum.value, whole)

    piece_rows = five[0].shape[0] // C
    norm_flat = norm_sum.value.astype(BF).reshape(-1)
    norm_columns = -(-norm_flat.size // (128 * piece_rows)) * 128
    norm_flat = jnp.pad(norm_flat, (0, piece_rows * norm_columns - norm_flat.size))
    norm_flat = jnp.broadcast_to(norm_flat.reshape(1, piece_rows, norm_columns), (C, piece_rows, norm_columns))
    enc_columns = enc_rows * width // piece_rows
    terms = jnp.concatenate(
        [value.reshape(C, piece_rows, width) for value in five]
        + [enc_term.reshape(C, piece_rows, enc_columns), norm_flat],
        2,
    )
    terms, whole = lax.optimization_barrier((terms, whole))
    whole = lax.all_gather(whole, "seq", axis=0, tiled=True)
    terms_got = exchanged(lambda owner: pick(terms, owner), "ctx")
    token = qkv.start(t6)
    terms = sum((after(value, token).astype(F32) for value in terms_got[1:]), terms_got[0].astype(F32))
    qkv_part = qkv.end(terms)
    five = terms[:, : 5 * width].astype(BF)
    grad_encoder = terms[:, 5 * width : 5 * width + enc_columns].reshape(enc_rows, width)
    norm_sums = terms[:, 5 * width + enc_columns :].reshape(-1)[: 6 * width // F].reshape(6, width // F)
    t7 = (five, qkv_part)

    def share_over_ctx(value):
        return [value] + [swap(value, "ctx", mask) for mask in range(1, C)]

    def stacked(got):
        if got[0].shape[0] % 16 == 0:
            return place(C * got[0].shape[0], got, lambda c_ref: [
                (c_ref[0] ^ mask) * got[0].shape[0] for mask in range(C)
            ], c_scalar)
        return by_owner_of(got, "ctx").reshape(-1, got[0].shape[1])

    five, qkv_part = lax.optimization_barrier((five, qkv_part))
    five_got, qkv_got = share_over_ctx(five), share_over_ctx(qkv_part)
    dqkv = columns_in_order([after(value, t7) for value in dqkv], 3)
    grad_input = d_r1 + dot_cols(dqkv, w_qkv)
    five = stacked([after(value, grad_input) for value in five_got])
    qkv_part = stacked([after(value, grad_input) for value in qkv_got])
    t8 = (five, qkv_part)

    five, qkv_part, whole = lax.optimization_barrier((five, qkv_part, whole))
    five_other, qkv_other = swap(five, "seq", 1), swap(qkv_part, "seq", 1)
    whole = whole.reshape(S * C, tile_rows, width)
    grad_ff_out = whole[:, : tile_rows // 2].reshape(-1, width).astype(F32)
    strips = whole[:, tile_rows // 2 :].reshape(S * C, F, -1, ff_width)
    strips = exchanged(lambda owner: pick(strips, owner, 1).reshape(-1, ff_width), "fsdp")
    grad_ff_in = line_up(strips, 1, f_scalar, F32)
    widths = [width, width, 2 * width, width]
    grad_cross_out, grad_cross_q, grad_cross_kv, grad_attn_out = two_halves(
        functools.partial(split_columns_kernel, widths),
        five, five_other, s_scalar, [(five.shape[0], size) for size in widths],
    )
    if head_width % 128 == 0:
        (grad_attn_qkv,) = two_halves(
            functools.partial(spread_parts_kernel, C, 3),
            qkv_part, qkv_other, s_scalar, [(qkv_part.shape[0] // C, 3 * width)],
        )
    else:
        both = jnp.where(s == 0, jnp.stack([qkv_part, qkv_other]), jnp.stack([qkv_other, qkv_part]))
        both = both.reshape(2, C, -1, 3, head_width).transpose(0, 2, 3, 1, 4)
        grad_attn_qkv = both.reshape(-1, 3 * width).astype(F32)
    return (
        mixed.reshape(1, rows, width),
        grad_input.reshape(1, rows, width),
        grad_encoder.reshape(1, enc_rows, width),
        grad_attn_qkv, grad_attn_out, grad_cross_q, grad_cross_kv, grad_cross_out,
        grad_ff_in, grad_ff_out, norm_sums[:3], norm_sums[3:],
    )


def solution(mesh):
    rows = P(("seq", "fsdp"), "ctx", None)
    shard = P("fsdp", None)
    columns = P(None, "fsdp")
    return jax.shard_map(
        functools.partial(local, mesh.shape["seq"], mesh.shape["ctx"], mesh.shape["fsdp"]),
        mesh=mesh,
        in_specs=(rows, rows) + (shard,) * 7 + (columns, columns, P(), rows),
        out_specs=(rows, rows, rows) + (shard,) * 7 + (columns, columns),
        check_vma=False,
    )
```

time: 1280 us -> 572 us (0.45)
  waiting for transfers between devices: 971 us -> 267 us
  matrix products: 156 us -> 79.6 us
  starting transfers between devices: 1.1 us -> 68.1 us
  Pallas kernels: 0 us -> 52.1 us
  blocking collectives: 32.9 us -> 0 us
    reduce_scatter x8 -> x3, waiting for transfers between devices: 395 us -> 17.2 us  [pair_sum_over(): lax.psum_scatter(value, axis, scatter_dimension=0, axis_index_groups=grou...]
    all_gather x9 -> x5, waiting for transfers between devices: 279 us -> 27.8 us  [the longest x1 18.1 us: local(): whole = lax.all_gather(part, 'ctx', axis=0, tiled=True)]
    psum x1 -> x0, waiting for transfers between devices: 247 us -> none  [local(): lax.psum(shards[0].astype(jnp.bfloat16), ('seq', 'ctx')).astype(jnp.float32)]
    ppermute x0 -> x78, waiting for transfers between devices: none -> 222 us  [the longest x72 193 us: swap(): lax.ppermute(value, axis, [(i, i ^ mask) for i in range(size_of[axis])])]
    dot_general x41 -> x48, matrix products: 156 us -> 79.6 us  [the longest x26 41.7 us: dot_rows(): lax.dot_general(left, right, (((0,), (0,)), ((), ())), preferred_element_...]
    ppermute x0 -> x78, starting transfers between devices: none -> 67.6 us  [the longest x72 63 us: swap(): lax.ppermute(value, axis, [(i, i ^ mask) for i in range(size_of[axis])])]
    pallas_call x0 -> x24, Pallas kernels: none -> 52.1 us  [the longest x2 15.9 us: attend_back(): pl.pallas_call(functools.partial(attend_back_kernel, causal, group // HEA...]
    unnamed x24 -> x8, waiting for transfers between devices: 50 us -> 0.81 us
  transfers between devices with their start and end apart: 21 -> 86, of which waited for: 18 -> 45; matrix products, arithmetic and copies ran while one was open for 14% -> 21% of each run, Pallas kernels for 0% -> 9%
where the time goes in v1:
time: 572 us; the launch traced here: 567 us
  waiting for transfers between devices  267 us (47%)
  matrix products  79.6 us (14%)
  starting transfers between devices  68.1 us (12%)
  local copies, waits for them, and re-layouts  61.1 us (11%)
  Pallas kernels  52.1 us (9%)
  other arithmetic  22.1 us (4%)
  between operations  16.2 us (3%)
    ppermute x72, waiting for transfers between devices, swap(): lax.ppermute(value, axis, [(i, i ^ mask) for i in range(size_of[axis])])  193 us
    ppermute x72, starting transfers between devices, swap(): lax.ppermute(value, axis, [(i, i ^ mask) for i in range(size_of[axis])])  63 us
    dot_general x26, matrix products, dot_rows(): lax.dot_general(left, right, (((0,), (0,)), ((), ())), preferred_element_...  41.7 us
    unnamed x295, local copies, waits for them, and re-layouts  37.9 us
    ppermute x6, waiting for transfers between devices, local(): lax.ppermute(v, 'ctx', [(i, (i + 1) % C) for i in range(C)])  28.5 us
    dot_general x9, matrix products, dot(): return jnp.dot(left, right, preferred_element_type=F32)  21.6 us
    all_gather x1, waiting for transfers between devices, local(): whole = lax.all_gather(part, 'ctx', axis=0, tiled=True)  18.1 us
    reduce_scatter x3, waiting for transfers between devices, pair_sum_over(): lax.psum_scatter(value, axis, scatter_dimension=0, axis_index_groups=grou...  17.2 us
  transfers between devices with their start and end apart: 86, of which 45 were waited for; matrix products, arithmetic and copies ran while one was open for 21% of the time, Pallas kernels for 9%

profile of v1, /device:TPU:0, one launch (start us, length us, event | category | flops | bytes accessed | tf_op | source)
XLA Modules:
  0.0 566.7 jit_solution(16222766970532092932)
XLA Ops:
  23.6 5.3 collective-permute-done.3.refs_4_
  34.0 9.3 %collective-permute-done.6.refs_7_ = bf16[128,1024]{1,0:T(8,128)(2,1)} collective-permute-done((bf16[128,1024]{1,0:T(8,128)(2,1)}, bf16[128,1024]{1,0:T(8,128)(2,1)}, u32[]{:S(2)}, u32[]{:S(2)}) %collective-permute-start.6) | collective-permute-done | bytes 262176 | tf_op jit(solution)/shard_map/ppermute | solution.py:489
  68.6 7.7 %shard_map.222 = (bf16[1024,256]{1,0:T(8,128)(2,1)S(1)}, f32[256,1024]{1,0:T(8,128)S(1)}, f32[8,1024]{1,0:T(8,128)S(1)}) custom-call(bf16[1024,768]{1,0:T(8,128)(2,1)S(1)} %convolution_convert_fusion.1.q_ref.k_ref.v_ref, bf16[1024,768]{1,0:T(8,128)(2,1)S(1)} %convolution_convert_fusion.1.q_ref.k_ref.v_ref, ...), custom_call_target="tpu_custom_call" | custom-call | flops 1073741824 | bytes 4194304 | tf_op jit(solution)/shard_map/pallas_call | solution.py:210
  106.9 5.8 %shard_map.226 = (bf16[256,1024]{1,0:T(8,128)(2,1)S(1)}, f32[1024,256]{1,0:T(8,128)S(1)}, f32[32,256]{1,0:T(8,128)S(1)}) custom-call(bf16[256,1024]{1,0:T(8,128)(2,1)S(1)} %copy-done.30, bf16[256,2048]{1,0:T(8,128)(2,1)S(1)} %convolution_convert_fusion.k_ref.v_ref, bf16[256,2048]{1,0:T(8,128)(2,1)S(1)} %convolution_convert_fusion.k_ref.v_ref), custom_call_target="tpu_custom_call" | custom-call | flops 268435456 | bytes 4194304 | tf_op jit(solution)/shard_map/pallas_call | solution.py:210
  114.5 9.7 %all-gather.10.cloned.1.call-done = bf16[1024,1024]{1,0:T(8,128)(2,1)} async-done(((bf16[256,1024]{1,0:T(8,128)(2,1)}), bf16[1024,1024]{1,0:T(8,128)(2,1)}) %all-gather.10.cloned.1.call-update) | async-done | bytes 2097168 | tf_op jit(solution)/shard_map/all_gather | solution.py:517
  133.5 8.5 %collective-permute-done.23 = bf16[256,1024]{1,0:T(8,128)(2,1)S(1)} collective-permute-done((bf16[256,1024]{1,0:T(8,128)(2,1)S(1)}, bf16[256,1024]{1,0:T(8,128)(2,1)S(1)}, u32[]{:S(2)}, u32[]{:S(2)}) %collective-permute-start.23) | collective-permute-done | bytes 524320 | tf_op jit(solution)/shard_map/ppermute | solution.py:396
  172.1 11.1 %collective-permute-done.29 = bf16[256,1024]{1,0:T(8,128)(2,1)S(1)} collective-permute-done((bf16[256,1024]{1,0:T(8,128)(2,1)S(1)}, bf16[256,1024]{1,0:T(8,128)(2,1)S(1)}, u32[]{:S(2)}, u32[]{:S(2)}) %collective-permute-start.29) | collective-permute-done | bytes 524320 | tf_op jit(solution)/shard_map/ppermute | solution.py:396
  213.7 5.8 %shard_map.233 = (bf16[256,1024]{1,0:T(8,128)(2,1)S(1)}, bf16[256,1024]{1,0:T(8,128)(2,1)S(1)}, bf16[256,1024]{1,0:T(8,128)(2,1)S(1)}) custom-call(bf16[256,1024]{1,0:T(8,128)(2,1)S(1)} %copy-done.31, bf16[256,2048]{1,0:T(8,128)(2,1)S(1)} %convolution_convert_fusion.k_ref.v_ref, bf16[256,2048]{1,0:T(8,128)(2,1)S(1)} %convolution_convert_fusion.k_ref.v_ref, ...), custom_call_target="tpu_custom_call" | custom-call | flops 671088640 | bytes 6291456 | tf_op jit(solution)/shard_map/pallas_call | solution.py:231
  230.8 19.0 %collective-permute-done.41.refs_3_ = bf16[256,3072]{1,0:T(8,128)(2,1)S(1)} collective-permute-done((bf16[256,3072]{1,0:T(8,128)(2,1)S(1)}, bf16[256,3072]{1,0:T(8,128)(2,1)S(1)}, u32[]{:S(2)}, u32[]{:S(2)}) %collective-permute-start.41) | collective-permute-done | bytes 1572896 | tf_op jit(solution)/shard_map/ppermute | solution.py:396
  274.1 10.2 %shard_map.235 = (bf16[1024,256]{1,0:T(8,128)(2,1)S(1)}, bf16[1024,256]{1,0:T(8,128)(2,1)S(1)}, bf16[1024,256]{1,0:T(8,128)(2,1)S(1)}) custom-call(bf16[1024,768]{1,0:T(8,128)(2,1)S(1)} %copy-done.63, bf16[1024,768]{1,0:T(8,128)(2,1)S(1)} %copy-done.63, bf16[1024,768]{1,0:T(8,128)(2,1)S(1)} %copy-done.63, bf16[1024,256]{1,0:T(8,128)(2,1)S(1)} %shard_map.234.do_ref, ...), custom_call_target="tpu_custom_call" | custom-call | flops 2684354560 | bytes 6291456 | tf_op jit(solution)/shard_map/pallas_call | solution.py:231
  293.1 5.3 collective-permute-start.46
  298.5 5.9 %collective-permute-done.51 = bf16[256,1024]{1,0:T(8,128)(2,1)S(1)} collective-permute-done((bf16[256,1024]{1,0:T(8,128)(2,1)}, bf16[256,1024]{1,0:T(8,128)(2,1)S(1)}, u32[]{:S(2)}, u32[]{:S(2)}) %collective-permute-start.51) | collective-permute-done | bytes 524320 | tf_op jit(solution)/shard_map/ppermute | solution.py:396
  315.6 9.0 %collective-permute-done.49 = bf16[256,1024]{1,0:T(8,128)(2,1)S(1)} collective-permute-done((bf16[256,1024]{1,0:T(8,128)(2,1)}, bf16[256,1024]{1,0:T(8,128)(2,1)S(1)}, u32[]{:S(2)}, u32[]{:S(2)}) %collective-permute-start.49) | collective-permute-done | bytes 524320 | tf_op jit(solution)/shard_map/ppermute | solution.py:396
  348.1 17.2 %reduce-scatter.8.cloned.1.call-done = bf16[256,1024]{1,0:T(8,128)(2,1)} async-done(((bf16[512,1024]{1,0:T(8,128)(2,1)}), bf16[256,1024]{1,0:T(8,128)(2,1)}) %reduce-scatter.8.cloned.1.call-update) | async-done | bytes 524304 | tf_op jit(solution)/shard_map/reduce_scatter | solution.py:722
  393.8 18.1 %all-gather.12.cloned.1.call-done = bf16[1024,1024]{1,0:T(8,128)(2,1)} async-done(((bf16[256,1024]{1,0:T(8,128)(2,1)}), bf16[1024,1024]{1,0:T(8,128)(2,1)}) %all-gather.12.cloned.1.call-update) | async-done | bytes 2097168 | tf_op jit(solution)/shard_map/all_gather | solution.py:784
  419.9 7.1 %collective-permute-done.62 = bf16[32,7296]{1,0:T(8,128)(2,1)S(1)} collective-permute-done((bf16[32,7296]{1,0:T(8,128)(2,1)S(1)}, bf16[32,7296]{1,0:T(8,128)(2,1)S(1)}, u32[]{:S(2)}, u32[]{:S(2)}) %collective-permute-start.62) | collective-permute-done | bytes 466976 | tf_op jit(solution)/shard_map/ppermute | solution.py:396
  427.0 10.5 %collective-permute-done.65 = bf16[32,7296]{1,0:T(8,128)(2,1)S(1)} collective-permute-done((bf16[32,7296]{1,0:T(8,128)(2,1)S(1)}, bf16[32,7296]{1,0:T(8,128)(2,1)S(1)}, u32[]{:S(2)}, u32[]{:S(2)}) %collective-permute-start.65) | collective-permute-done | bytes 466976 | tf_op jit(solution)/shard_map/ppermute | solution.py:396
  437.5 19.5 %collective-permute-done.64 = bf16[32,7296]{1,0:T(8,128)(2,1)S(1)} collective-permute-done((bf16[32,7296]{1,0:T(8,128)(2,1)S(1)}, bf16[32,7296]{1,0:T(8,128)(2,1)S(1)}, u32[]{:S(2)}, u32[]{:S(2)}) %collective-permute-start.64) | collective-permute-done | bytes 466976 | tf_op jit(solution)/shard_map/ppermute | solution.py:396
  473.9 5.6 convolution_add_fusion.8
  479.5 10.8 %collective-permute-done.71.refs_3_ = bf16[128,768]{1,0:T(8,128)(2,1)S(1)} collective-permute-done((bf16[128,768]{1,0:T(8,128)(2,1)S(1)}, bf16[128,768]{1,0:T(8,128)(2,1)S(1)}, u32[]{:S(2)}, u32[]{:S(2)}) %collective-permute-start.71) | collective-permute-done | bytes 196640 | tf_op jit(solution)/shard_map/ppermute | solution.py:396
  491.3 13.9 %collective-permute-done.68.refs_3_ = bf16[32,5120]{1,0:T(8,128)(2,1)S(1)} collective-permute-done((bf16[32,5120]{1,0:T(8,128)(2,1)S(1)}, bf16[32,5120]{1,0:T(8,128)(2,1)S(1)}, u32[]{:S(2)}, u32[]{:S(2)}) %collective-permute-start.68) | collective-permute-done | bytes 327712 | tf_op jit(solution)/shard_map/ppermute | solution.py:396
  524.2 5.2 collective-permute-done.76.refs_2_
  530.2 7.6 %collective-permute-done.77.refs_3_ = bf16[256,1024]{1,0:T(8,128)(2,1)S(1)} collective-permute-done((bf16[256,1024]{1,0:T(8,128)(2,1)}, bf16[256,1024]{1,0:T(8,128)(2,1)S(1)}, u32[]{:S(2)}, u32[]{:S(2)}) %collective-permute-start.77) | collective-permute-done | bytes 524320 | tf_op jit(solution)/shard_map/ppermute | solution.py:396
  544.7 7.9 %collective-permute-done.73.other_ref = bf16[512,768]{1,0:T(8,128)(2,1)} collective-permute-done((bf16[512,768]{1,0:T(8,128)(2,1)}, bf16[512,768]{1,0:T(8,128)(2,1)}, u32[]{:S(2)}, u32[]{:S(2)}) %collective-permute-start.73) | collective-permute-done | bytes 786464 | tf_op jit(solution)/shard_map/ppermute | solution.py:396
  (605 shorter events, 314.5 us)
Async XLA Ops:
  7.2 92.7 %all-gather.6.cloned.1.call-start = ((), (), s32[]{:S(2)}) async-start(), calls=%async_computation.3 | async-start | bytes 2621440 | tf_op jit(solution)/shard_map/all_gather | solution.py:517
  31.1 72.1 %all-gather.8.cloned.1.call-start = ((), (), s32[]{:S(2)}) async-start(), calls=%async_computation.4 | async-start | bytes 5242880 | tf_op jit(solution)/shard_map/all_gather | solution.py:517
  31.9 92.4 %all-gather.10.cloned.1.call-start = ((), (), s32[]{:S(2)}) async-start(), calls=%async_computation.5 | async-start | bytes 2621440 | tf_op jit(solution)/shard_map/all_gather | solution.py:517
  49.0 217.5 %reduce-scatter.4.cloned.1.call-start = ((), (), s32[]{:S(2)}) async-start(), calls=%async_computation.6 | async-start | bytes 6291456 | tf_op jit(solution)/shard_map/reduce_scatter | solution.py:722
  49.8 46.0 %collective-permute-start.14 = (bf16[256,1024]{1,0:T(8,128)(2,1)S(1)}, bf16[256,1024]{1,0:T(8,128)(2,1)}, u32[]{:S(2)}, u32[]{:S(2)}) collective-permute-start(bf16[256,1024]{1,0:T(8,128)(2,1)S(1)} %copy-done.39), channel_id=1, source_target_pairs={{0,1},{1,0},{2,3},{3,2},{4,5},{5,4},{6,7},{7,6},{8,9},{9,8},{10,11... | collective-permute-start | bytes 1572872 | tf_op jit(solution)/shard_map/ppermute | solution.py:396
  89.0 39.2 %collective-permute-start.22 = (bf16[256,1024]{1,0:T(8,128)(2,1)}, bf16[256,1024]{1,0:T(8,128)(2,1)}, u32[]{:S(2)}, u32[]{:S(2)}) collective-permute-start(bf16[256,1024]{1,0:T(8,128)(2,1)} %get-tuple-element.402), channel_id=1, source_target_pairs={{0,3},{1,2},{2,1},{3,0},{4,7},{5,6},{6,5},{7,4},{8,11},{9,10},{10,... | collective-permute-start | bytes 1572872 | tf_op jit(solution)/shard_map/ppermute | solution.py:396
  202.3 125.0 %reduce-scatter.6.cloned.1.call-start = ((), (), s32[]{:S(2)}) async-start(), calls=%async_computation.7 | async-start | bytes 3145728 | tf_op jit(solution)/shard_map/reduce_scatter | solution.py:722
  212.9 36.8 %collective-permute-start.41 = (bf16[256,3072]{1,0:T(8,128)(2,1)S(1)}, bf16[256,3072]{1,0:T(8,128)(2,1)S(1)}, u32[]{:S(2)}, u32[]{:S(2)}) collective-permute-start(bf16[256,3072]{1,0:T(8,128)(2,1)S(1)} %copy-done.17), channel_id=1, source_target_pairs={{0,2},{1,3},{2,0},{3,1},{4,6},{5,7},{6,4},{7,5},{8,10},{9,11},{10,... | collective-permute-start | bytes 4718600 | tf_op jit(solution)/shard_map/ppermute | solution.py:396
  213.5 36.2 %collective-permute-start.40 = (bf16[256,3072]{1,0:T(8,128)(2,1)S(1)}, bf16[256,3072]{1,0:T(8,128)(2,1)S(1)}, u32[]{:S(2)}, u32[]{:S(2)}) collective-permute-start(bf16[256,3072]{1,0:T(8,128)(2,1)S(1)} %copy-done.17), channel_id=1, source_target_pairs={{0,1},{1,0},{2,3},{3,2},{4,5},{5,4},{6,7},{7,6},{8,9},{9,8},{10,11... | collective-permute-start | bytes 4718600 | tf_op jit(solution)/shard_map/ppermute | solution.py:396
  266.5 98.8 %reduce-scatter.8.cloned.1.call-start = ((), (), s32[]{:S(2)}) async-start(), calls=%async_computation.8 | async-start | bytes 1572864 | tf_op jit(solution)/shard_map/reduce_scatter | solution.py:722
  268.8 35.5 %collective-permute-start.51 = (bf16[256,1024]{1,0:T(8,128)(2,1)}, bf16[256,1024]{1,0:T(8,128)(2,1)S(1)}, u32[]{:S(2)}, u32[]{:S(2)}) collective-permute-start(bf16[256,1024]{1,0:T(8,128)(2,1)} %fusion.54), channel_id=1, source_target_pairs={{0,2},{1,3},{2,0},{3,1},{4,6},{5,7},{6,4},{7,5},{8,10},{9,11},{10,... | collective-permute-start | bytes 1572872 | tf_op jit(solution)/shard_map/ppermute | solution.py:396
  269.4 46.2 %collective-permute-start.50 = (bf16[256,1024]{1,0:T(8,128)(2,1)}, bf16[256,1024]{1,0:T(8,128)(2,1)S(1)}, u32[]{:S(2)}, u32[]{:S(2)}) collective-permute-start(bf16[256,1024]{1,0:T(8,128)(2,1)} %fusion.53), channel_id=1, source_target_pairs={{0,2},{1,3},{2,0},{3,1},{4,6},{5,7},{6,4},{7,5},{8,10},{9,11},{10,... | collective-permute-start | bytes 1572872 | tf_op jit(solution)/shard_map/ppermute | solution.py:396
  270.9 53.7 %collective-permute-start.49 = (bf16[256,1024]{1,0:T(8,128)(2,1)}, bf16[256,1024]{1,0:T(8,128)(2,1)S(1)}, u32[]{:S(2)}, u32[]{:S(2)}) collective-permute-start(bf16[256,1024]{1,0:T(8,128)(2,1)} %fusion.52), channel_id=1, source_target_pairs={{0,2},{1,3},{2,0},{3,1},{4,6},{5,7},{6,4},{7,5},{8,10},{9,11},{10,... | collective-permute-start | bytes 1572872 | tf_op jit(solution)/shard_map/ppermute | solution.py:396
  285.1 39.4 %collective-permute-start.45 = (bf16[256,768]{1,0:T(8,128)(2,1)S(1)}, bf16[256,768]{1,0:T(8,128)(2,1)S(1)}, u32[]{:S(2)}, u32[]{:S(2)}) collective-permute-start(bf16[256,768]{1,0:T(8,128)(2,1)S(1)} %get-tuple-element.268), channel_id=1, source_target_pairs={{0,4},{4,0},{8,12},{12,8},{1,5},{5,1},{9,13},{13,9},{2,6},{6,2},{1... | collective-permute-start | bytes 1179656 | tf_op jit(solution)/shard_map/ppermute | solution.py:396
  327.3 84.6 %all-gather.12.cloned.1.call-start = ((), (), s32[]{:S(2)}) async-start(), calls=%async_computation.9 | async-start | bytes 2621440 | tf_op jit(solution)/shard_map/all_gather | solution.py:784
  332.7 38.9 %collective-permute-start.61 = (f32[1,6,256]{2,0,1:T(1,128)S(1)}, f32[1,6,256]{2,0,1:T(1,128)S(1)}, u32[]{:S(2)}, u32[]{:S(2)}) collective-permute-start(f32[1,6,256]{2,0,1:T(1,128)S(1)} %dynamic-slice_add_fusion), channel_id=1, source_target_pairs={{0,16},{16,0},{1,17},{17,1},{2,18},{18,2},{3,19},{19,3},{4,20},{20... | collective-permute-start | bytes 18440 | tf_op jit(solution)/shard_map/ppermute | solution.py:396
  341.5 37.0 %collective-permute-start.55 = (bf16[128,1024]{1,0:T(8,128)(2,1)}, bf16[128,1024]{1,0:T(8,128)(2,1)}, u32[]{:S(2)}, u32[]{:S(2)}) collective-permute-start(bf16[128,1024]{1,0:T(8,128)(2,1)} %fusion.73), channel_id=1, source_target_pairs={{0,16},{16,0},{1,17},{17,1},{2,18},{18,2},{3,19},{19,3},{4,20},{20... | collective-permute-start | bytes 786440 | tf_op jit(solution)/shard_map/ppermute | solution.py:396
  365.3 140.0 %all-gather.14.cloned.1.call-start = ((), (), s32[]{:S(2)}) async-start(), calls=%async_computation.10 | async-start | bytes 6291456 | tf_op jit(solution)/shard_map/all_gather | solution.py:805
  377.0 39.8 %collective-permute-start.63 = (bf16[256,768]{1,0:T(8,128)(2,1)}, bf16[256,768]{1,0:T(8,128)(2,1)}, u32[]{:S(2)}, u32[]{:S(2)}) collective-permute-start(bf16[256,768]{1,0:T(8,128)(2,1)} %fusion.56), channel_id=1, source_target_pairs={{0,2},{1,3},{2,0},{3,1},{4,6},{5,7},{6,4},{7,5},{8,10},{9,11},{10,... | collective-permute-start | bytes 1179656 | tf_op jit(solution)/shard_map/ppermute | solution.py:396
  415.9 41.1 %collective-permute-start.64 = (bf16[32,7296]{1,0:T(8,128)(2,1)S(1)}, bf16[32,7296]{1,0:T(8,128)(2,1)S(1)}, u32[]{:S(2)}, u32[]{:S(2)}) collective-permute-start(bf16[32,7296]{1,0:T(8,128)(2,1)S(1)} %get-tuple-element.408), channel_id=1, source_target_pairs={{0,8},{4,12},{8,0},{12,4},{1,9},{5,13},{9,1},{13,5},{2,10},{6,14},... | collective-permute-start | bytes 1400840 | tf_op jit(solution)/shard_map/ppermute | solution.py:396
  418.4 40.7 %collective-permute-start.66 = (bf16[128,768]{1,0:T(8,128)(2,1)S(1)}, bf16[128,768]{1,0:T(8,128)(2,1)S(1)}, u32[]{:S(2)}, u32[]{:S(2)}) collective-permute-start(bf16[128,768]{1,0:T(8,128)(2,1)S(1)} %fusion.85), channel_id=1, source_target_pairs={{0,16},{16,0},{1,17},{17,1},{2,18},{18,2},{3,19},{19,3},{4,20},{20... | collective-permute-start | bytes 589832 | tf_op jit(solution)/shard_map/ppermute | solution.py:396
  466.5 38.7 %collective-permute-start.68 = (bf16[32,5120]{1,0:T(8,128)(2,1)S(1)}, bf16[32,5120]{1,0:T(8,128)(2,1)S(1)}, u32[]{:S(2)}, u32[]{:S(2)}) collective-permute-start(bf16[32,5120]{1,0:T(8,128)(2,1)S(1)} %slice.527.refs_1_), channel_id=1, source_target_pairs={{0,8},{4,12},{8,0},{12,4},{1,9},{5,13},{9,1},{13,5},{2,10},{6,14},... | collective-permute-start | bytes 983048 | tf_op jit(solution)/shard_map/ppermute | solution.py:396
  505.3 50.4 %collective-permute-start.74 = (bf16[128,5120]{1,0:T(8,128)(2,1)S(1)}, bf16[128,5120]{1,0:T(8,128)(2,1)}, u32[]{:S(2)}, u32[]{:S(2)}) collective-permute-start(bf16[128,5120]{1,0:T(8,128)(2,1)S(1)} %shard_map.239.own_ref), channel_id=1, source_target_pairs={{0,16},{16,0},{1,17},{17,1},{2,18},{18,2},{3,19},{19,3},{4,20},{20... | collective-permute-start | bytes 3932168 | tf_op jit(solution)/shard_map/ppermute | solution.py:396
  508.5 44.1 %collective-permute-start.73 = (bf16[512,768]{1,0:T(8,128)(2,1)}, bf16[512,768]{1,0:T(8,128)(2,1)}, u32[]{:S(2)}, u32[]{:S(2)}) collective-permute-start(bf16[512,768]{1,0:T(8,128)(2,1)} %copy-done.15), channel_id=1, source_target_pairs={{0,16},{16,0},{1,17},{17,1},{2,18},{18,2},{3,19},{19,3},{4,20},{20... | collective-permute-start | bytes 2359304 | tf_op jit(solution)/shard_map/ppermute | solution.py:396
  (198 other events, 2024.0 us)
Sparse Core Ops, SparseCore 0:
  31.2 21.0 all-gather.5
  53.8 34.7 all-gather.7
  90.2 33.9 all-gather.9
  202.4 55.0 reduce-scatter.3
  266.6 50.7 reduce-scatter.5
  327.4 37.8 reduce-scatter.7
  366.9 44.9 all-gather.11
  413.5 55.9 all-gather.13

commit v2 on v1

--- a/solution.py
+++ b/solution.py
@@ -699,29 +699,17 @@
     tile_ff_in = joined([after(value, sent) for value in h_2_rows], d_pres)
     tile_ff_out = joined([after(act, sent) for act in acts], df_rows)
     tile_ff_in, tile_ff_out = lax.optimization_barrier((tile_ff_in, tile_ff_out))
-    def turned_chunks(value):
-        split = [2] * (C.bit_length() - 1)
-        view = value.reshape(S, *split, *value.shape[1:])
-        axes = (0, *range(len(split), 0, -1), len(split) + 1, len(split) + 2)
-        return view.transpose(*axes).reshape(value.shape)
-
     tiles = jnp.concatenate(
         [
-            turned_chunks(tile_ff_out.reshape(S * C, -1, width)),
-            turned_chunks(
-                tile_ff_in.reshape(F, S * C, -1, ff_width).transpose(1, 0, 2, 3).reshape(S * C, -1, width)
-            ),
+            tile_ff_out.reshape(S * C, -1, width),
+            tile_ff_in.reshape(F, S * C, -1, ff_width).transpose(1, 0, 2, 3).reshape(S * C, -1, width),
         ],
         1,
     )
     tile_rows = tiles.shape[1]
     d_h2 = d_r3 + finish((tiles,))
 
-    def pair_sum_over(value, axis, bit):
-        groups = [[i, i | bit] for i in range(size_of[axis]) if not i & bit]
-        return lax.psum_scatter(value, axis, scatter_dimension=0, axis_index_groups=groups, tiled=True)
-
-    part = pair_sum_over(tiles.reshape(-1, width), "seq", 1)
+    part = lax.psum_scatter(tiles.reshape(-1, width), ("seq", "ctx"), scatter_dimension=0, tiled=True)
 
     qkv_shards = spread(after(attn_qkv, d_h2))
     d_r2, d_gain_1, d_shift_1 = norm_back(d_h2, unit_1, scale_1, gains[1])
@@ -739,7 +727,12 @@
     d_att_got = [d_att_pieces[0]] + [swap(d_att_pieces[mask], "ctx", mask) for mask in range(1, C)]
     t3 = (d_att_pieces, d_att_got[1] if C > 1 else ())
     fsdp_rest = len(rest_of["fsdp"])
-    norm_terms = jnp.concatenate([d_gain_0, d_gain_1, d_gain_2, d_shift_0, d_shift_1, d_shift_2], 0)
+    def join_rows(*refs):
+        for row, ref in enumerate(refs[:-1]):
+            refs[-1][row : row + 1, :] = ref[...]
+
+    norm_terms = [d_gain_0, d_gain_1, d_gain_2, d_shift_0, d_shift_1, d_shift_2]
+    norm_terms = moved(join_rows, [], norm_terms, [(6, width)], F32)[0]
     norm_sum = Sum(norm_terms.reshape(6, F, width // F).transpose(1, 0, 2), F32)
     norm_sum.start("fsdp", first_of["fsdp"], t3)
     cq_, ck, cv, ao = (
@@ -760,8 +753,6 @@
     enc_term = enc_term.astype(BF)
     d_att = to_columns([after(value, token, enc_term, qkv_shards) for value in d_att_got])
 
-    d_att, part = lax.optimization_barrier((d_att, part))
-    part = pair_sum_over(part, "ctx", 1)
     dq, dk, dv = attend_back(True, *self_in, d_att, att_t, att_lse, head_width, self_parts)
     dqkv_mine = jnp.concatenate([dq, dk, dv], 1)
 
@@ -779,8 +770,6 @@
     dqkv = to_rows(dqkv_mine)
     gots = (co.got, cq_.got, ck.got, cv.got, ao.got)
     dqkv, w_qkv, gots, part = lax.optimization_barrier((dqkv, w_qkv, gots, part))
-    for bit in rest_of["ctx"]:
-        part = pair_sum_over(part, "ctx", bit)
     whole = lax.all_gather(part, "ctx", axis=0, tiled=True)
     for one, got in zip((co, cq_, ck, cv, ao), gots):
         one.got = got

time: 572 us -> 535 us (0.935)
  waiting for transfers between devices: 267 us -> 234 us
  local copies, waits for them, and re-layouts: 61.1 us -> 50.9 us
    reduce_scatter x3 -> x1, waiting for transfers between devices: 17.2 us -> 0.01 us  [local(): lax.psum_scatter(tiles.reshape(-1, width), ('seq', 'ctx'), scatter_dimens...]
    all_gather x1, waiting for transfers between devices: 18.1 us -> 2.78 us  [local(): whole = lax.all_gather(part, 'ctx', axis=0, tiled=True)]
    unnamed x295 -> x286, local copies, waits for them, and re-layouts: 37.9 us -> 27.4 us
    pallas_call x18 -> x19, Pallas kernels: 15.7 us -> 18.6 us  [moved(): pl.pallas_call(kernel, in_specs=[SMEM] * len(scalars) + [IN_VMEM] * len(v...]
  transfers between devices with their start and end apart: 86 -> 84, of which waited for: 45 -> 39; matrix products, arithmetic and copies ran while one was open for 21% -> 23% of each run, Pallas kernels for 9% -> 10%
where the time goes in v2:
time: 535 us; the launch traced here: 530 us
  waiting for transfers between devices  234 us (44%)
  matrix products  81.1 us (15%)
  starting transfers between devices  67.7 us (13%)
  Pallas kernels  55 us (10%)
  local copies, waits for them, and re-layouts  50.9 us (10%)
  other arithmetic  25.7 us (5%)
  between operations  16.1 us (3%)
    ppermute x72, waiting for transfers between devices, swap(): lax.ppermute(value, axis, [(i, i ^ mask) for i in range(size_of[axis])])  193 us
    ppermute x72, starting transfers between devices, swap(): lax.ppermute(value, axis, [(i, i ^ mask) for i in range(size_of[axis])])  62.6 us
    dot_general x26, matrix products, dot_rows(): lax.dot_general(left, right, (((0,), (0,)), ((), ())), preferred_element_...  40.8 us
    ppermute x6, waiting for transfers between devices, local(): lax.ppermute(v, 'ctx', [(i, (i + 1) % C) for i in range(C)])  28.5 us
    unnamed x286, local copies, waits for them, and re-layouts  27.4 us
    dot_general x9, matrix products, dot(): return jnp.dot(left, right, preferred_element_type=F32)  21.6 us
    dot_general x13, matrix products, dot_cols(): lax.dot_general(left, right, (((1,), (1,)), ((), ())), preferred_element_...  18.7 us
    pallas_call x19, Pallas kernels, moved(): pl.pallas_call(kernel, in_specs=[SMEM] * len(scalars) + [IN_VMEM] * len(v...  18.6 us
  transfers between devices with their start and end apart: 84, of which 39 were waited for; matrix products, arithmetic and copies ran while one was open for 23% of the time, Pallas kernels for 10%

profile of v2, /device:TPU:0, one launch (start us, length us, event | category | flops | bytes accessed | tf_op | source)
XLA Modules:
  0.0 530.1 jit_solution(18111315514126122534)
XLA Ops:
  34.0 9.3 %collective-permute-done.6.refs_7_ = bf16[128,1024]{1,0:T(8,128)(2,1)} collective-permute-done((bf16[128,1024]{1,0:T(8,128)(2,1)}, bf16[128,1024]{1,0:T(8,128)(2,1)}, u32[]{:S(2)}, u32[]{:S(2)}) %collective-permute-start.6) | collective-permute-done | bytes 262176 | tf_op jit(solution)/shard_map/ppermute | solution.py:489
  68.6 7.7 %shard_map.222 = (bf16[1024,256]{1,0:T(8,128)(2,1)S(1)}, f32[256,1024]{1,0:T(8,128)S(1)}, f32[8,1024]{1,0:T(8,128)S(1)}) custom-call(bf16[1024,768]{1,0:T(8,128)(2,1)S(1)} %convolution_convert_fusion.1.q_ref.k_ref.v_ref, bf16[1024,768]{1,0:T(8,128)(2,1)S(1)} %convolution_convert_fusion.1.q_ref.k_ref.v_ref, ...), custom_call_target="tpu_custom_call" | custom-call | flops 1073741824 | bytes 4194304 | tf_op jit(solution)/shard_map/pallas_call | solution.py:210
  80.6 6.6 %collective-permute-done.11.refs_1_ = bf16[256,256]{1,0:T(8,128)(2,1)S(1)} collective-permute-done((bf16[256,256]{1,0:T(8,128)(2,1)S(1)}, bf16[256,256]{1,0:T(8,128)(2,1)S(1)}, u32[]{:S(2)}, u32[]{:S(2)}) %collective-permute-start.11) | collective-permute-done | bytes 131104 | tf_op jit(solution)/shard_map/ppermute | solution.py:396
  89.4 5.7 %collective-permute-done.13.refs_3_ = bf16[256,256]{1,0:T(8,128)(2,1)S(1)} collective-permute-done((bf16[256,256]{1,0:T(8,128)(2,1)S(1)}, bf16[256,256]{1,0:T(8,128)(2,1)S(1)}, u32[]{:S(2)}, u32[]{:S(2)}) %collective-permute-start.13) | collective-permute-done | bytes 131104 | tf_op jit(solution)/shard_map/ppermute | solution.py:396
  107.8 5.8 %shard_map.226 = (bf16[256,1024]{1,0:T(8,128)(2,1)S(1)}, f32[1024,256]{1,0:T(8,128)S(1)}, f32[32,256]{1,0:T(8,128)S(1)}) custom-call(bf16[256,1024]{1,0:T(8,128)(2,1)S(1)} %copy-done.30, bf16[256,2048]{1,0:T(8,128)(2,1)S(1)} %convolution_convert_fusion.k_ref.v_ref, bf16[256,2048]{1,0:T(8,128)(2,1)S(1)} %convolution_convert_fusion.k_ref.v_ref), custom_call_target="tpu_custom_call" | custom-call | flops 268435456 | bytes 4194304 | tf_op jit(solution)/shard_map/pallas_call | solution.py:210
  115.4 8.8 %all-gather.10.cloned.1.call-done = bf16[1024,1024]{1,0:T(8,128)(2,1)} async-done(((bf16[256,1024]{1,0:T(8,128)(2,1)}), bf16[1024,1024]{1,0:T(8,128)(2,1)}) %all-gather.10.cloned.1.call-update) | async-done | bytes 2097168 | tf_op jit(solution)/shard_map/all_gather | solution.py:517
  133.5 8.5 %collective-permute-done.23 = bf16[256,1024]{1,0:T(8,128)(2,1)S(1)} collective-permute-done((bf16[256,1024]{1,0:T(8,128)(2,1)S(1)}, bf16[256,1024]{1,0:T(8,128)(2,1)S(1)}, u32[]{:S(2)}, u32[]{:S(2)}) %collective-permute-start.23) | collective-permute-done | bytes 524320 | tf_op jit(solution)/shard_map/ppermute | solution.py:396
  173.1 10.2 %collective-permute-done.29 = bf16[256,1024]{1,0:T(8,128)(2,1)S(1)} collective-permute-done((bf16[256,1024]{1,0:T(8,128)(2,1)S(1)}, bf16[256,1024]{1,0:T(8,128)(2,1)S(1)}, u32[]{:S(2)}, u32[]{:S(2)}) %collective-permute-start.29) | collective-permute-done | bytes 524320 | tf_op jit(solution)/shard_map/ppermute | solution.py:396
  216.5 5.8 %shard_map.233 = (bf16[256,1024]{1,0:T(8,128)(2,1)S(1)}, bf16[256,1024]{1,0:T(8,128)(2,1)S(1)}, bf16[256,1024]{1,0:T(8,128)(2,1)S(1)}) custom-call(bf16[256,1024]{1,0:T(8,128)(2,1)S(1)} %copy-done.31, bf16[256,2048]{1,0:T(8,128)(2,1)S(1)} %convolution_convert_fusion.k_ref.v_ref, bf16[256,2048]{1,0:T(8,128)(2,1)S(1)} %convolution_convert_fusion.k_ref.v_ref, ...), custom_call_target="tpu_custom_call" | custom-call | flops 671088640 | bytes 6291456 | tf_op jit(solution)/shard_map/pallas_call | solution.py:231
  230.9 7.9 %collective-permute-done.34 = bf16[256,256]{1,0:T(8,128)(2,1)} collective-permute-done((bf16[256,256]{1,0:T(8,128)(2,1)}, bf16[256,256]{1,0:T(8,128)(2,1)}, u32[]{:S(2)}, u32[]{:S(2)}) %collective-permute-start.34) | collective-permute-done | bytes 131104 | tf_op jit(solution)/shard_map/ppermute | solution.py:396
  242.6 10.5 %collective-permute-done.41.refs_3_ = bf16[256,3072]{1,0:T(8,128)(2,1)} collective-permute-done((bf16[256,3072]{1,0:T(8,128)(2,1)}, bf16[256,3072]{1,0:T(8,128)(2,1)}, u32[]{:S(2)}, u32[]{:S(2)}) %collective-permute-start.41) | collective-permute-done | bytes 1572896 | tf_op jit(solution)/shard_map/ppermute | solution.py:396
  274.1 10.2 %shard_map.235 = (bf16[1024,256]{1,0:T(8,128)(2,1)S(1)}, bf16[1024,256]{1,0:T(8,128)(2,1)S(1)}, bf16[1024,256]{1,0:T(8,128)(2,1)S(1)}) custom-call(bf16[1024,768]{1,0:T(8,128)(2,1)S(1)} %copy-done.55, bf16[1024,768]{1,0:T(8,128)(2,1)S(1)} %copy-done.55, bf16[1024,768]{1,0:T(8,128)(2,1)S(1)} %copy-done.55, bf16[1024,256]{1,0:T(8,128)(2,1)S(1)} %shard_map.234.do_ref, ...), custom_call_target="tpu_custom_call" | custom-call | flops 2684354560 | bytes 6291456 | tf_op jit(solution)/shard_map/pallas_call | solution.py:231
  291.7 9.6 %collective-permute-done.51 = bf16[256,1024]{1,0:T(8,128)(2,1)S(1)} collective-permute-done((bf16[256,1024]{1,0:T(8,128)(2,1)}, bf16[256,1024]{1,0:T(8,128)(2,1)S(1)}, u32[]{:S(2)}, u32[]{:S(2)}) %collective-permute-start.51) | collective-permute-done | bytes 524320 | tf_op jit(solution)/shard_map/ppermute | solution.py:396
  303.8 6.1 %shard_map.237 = bf16[1024,3072]{1,0:T(8,128)(2,1)} custom-call(s32[1]{0:T(128)} %bitcast.4.refs_0_.at_ref, bf16[256,3072]{1,0:T(8,128)(2,1)} %refs_1_.7, bf16[256,3072]{1,0:T(8,128)(2,1)} %collective-permute-done.40.refs_2_, bf16[256,3072]{1,0:T(8,128)(2,1)} %collective-permute-done.41.refs_3_, bf16[256,3072]{1,0:T(8,128)(2,1)} %collective-permute-done.42.refs_4_), custom_call_target="tpu_custom_call" | custom-call | bytes 12582912 | tf_op jit(solution)/shard_map/pallas_call | solution.py:255
  314.0 8.0 %collective-permute-done.49 = bf16[256,1024]{1,0:T(8,128)(2,1)S(1)} collective-permute-done((bf16[256,1024]{1,0:T(8,128)(2,1)S(1)}, bf16[256,1024]{1,0:T(8,128)(2,1)S(1)}, u32[]{:S(2)}, u32[]{:S(2)}) %collective-permute-start.49) | collective-permute-done | bytes 524320 | tf_op jit(solution)/shard_map/ppermute | solution.py:396
  344.0 11.6 %collective-permute-done.58 = bf16[128,1024]{1,0:T(8,128)(2,1)} collective-permute-done((bf16[128,1024]{1,0:T(8,128)(2,1)}, bf16[128,1024]{1,0:T(8,128)(2,1)}, u32[]{:S(2)}, u32[]{:S(2)}) %collective-permute-start.58) | collective-permute-done | bytes 262176 | tf_op jit(solution)/shard_map/ppermute | solution.py:396
  385.7 13.4 %collective-permute-done.62 = bf16[32,7296]{1,0:T(8,128)(2,1)S(1)} collective-permute-done((bf16[32,7296]{1,0:T(8,128)(2,1)S(1)}, bf16[32,7296]{1,0:T(8,128)(2,1)S(1)}, u32[]{:S(2)}, u32[]{:S(2)}) %collective-permute-start.62) | collective-permute-done | bytes 466976 | tf_op jit(solution)/shard_map/ppermute | solution.py:396
  403.8 18.0 %collective-permute-done.64 = bf16[32,7296]{1,0:T(8,128)(2,1)S(1)} collective-permute-done((bf16[32,7296]{1,0:T(8,128)(2,1)S(1)}, bf16[32,7296]{1,0:T(8,128)(2,1)S(1)}, u32[]{:S(2)}, u32[]{:S(2)}) %collective-permute-start.64) | collective-permute-done | bytes 466976 | tf_op jit(solution)/shard_map/ppermute | solution.py:396
  434.8 6.1 %collective-permute-start.67 = (bf16[32,5120]{1,0:T(8,128)(2,1)S(1)}, bf16[32,5120]{1,0:T(8,128)(2,1)S(1)}, u32[]{:S(2)}, u32[]{:S(2)}) collective-permute-start(bf16[32,5120]{1,0:T(8,128)(2,1)S(1)} %slice.527.refs_1_), channel_id=1, source_target_pairs={{0,4},{4,0},{8,12},{12,8},{1,5},{5,1},{9,13},{13,9},{2,6},{6,2},{1... | collective-permute-start | bytes 983048 | tf_op jit(solution)/shard_map/ppermute | solution.py:396
  446.4 9.6 %collective-permute-done.71.refs_3_ = bf16[128,768]{1,0:T(8,128)(2,1)S(1)} collective-permute-done((bf16[128,768]{1,0:T(8,128)(2,1)S(1)}, bf16[128,768]{1,0:T(8,128)(2,1)S(1)}, u32[]{:S(2)}, u32[]{:S(2)}) %collective-permute-start.71) | collective-permute-done | bytes 196640 | tf_op jit(solution)/shard_map/ppermute | solution.py:396
  456.1 13.3 %collective-permute-done.68.refs_3_ = bf16[32,5120]{1,0:T(8,128)(2,1)S(1)} collective-permute-done((bf16[32,5120]{1,0:T(8,128)(2,1)S(1)}, bf16[32,5120]{1,0:T(8,128)(2,1)S(1)}, u32[]{:S(2)}, u32[]{:S(2)}) %collective-permute-start.68) | collective-permute-done | bytes 327712 | tf_op jit(solution)/shard_map/ppermute | solution.py:396
  485.0 6.9 %collective-permute-done.76.refs_2_ = bf16[256,1024]{1,0:T(8,128)(2,1)S(1)} collective-permute-done((bf16[256,1024]{1,0:T(8,128)(2,1)}, bf16[256,1024]{1,0:T(8,128)(2,1)S(1)}, u32[]{:S(2)}, u32[]{:S(2)}) %collective-permute-start.76) | collective-permute-done | bytes 524320 | tf_op jit(solution)/shard_map/ppermute | solution.py:396
  492.7 6.1 %collective-permute-done.77.refs_3_ = bf16[256,1024]{1,0:T(8,128)(2,1)} collective-permute-done((bf16[256,1024]{1,0:T(8,128)(2,1)}, bf16[256,1024]{1,0:T(8,128)(2,1)}, u32[]{:S(2)}, u32[]{:S(2)}) %collective-permute-start.77) | collective-permute-done | bytes 524320 | tf_op jit(solution)/shard_map/ppermute | solution.py:396
  503.4 12.7 %collective-permute-done.73.other_ref = bf16[512,768]{1,0:T(8,128)(2,1)} collective-permute-done((bf16[512,768]{1,0:T(8,128)(2,1)S(1)}, bf16[512,768]{1,0:T(8,128)(2,1)}, u32[]{:S(2)}, u32[]{:S(2)}) %collective-permute-start.73) | collective-permute-done | bytes 786464 | tf_op jit(solution)/shard_map/ppermute | solution.py:396
  (584 shorter events, 295.8 us)
Async XLA Ops:
  7.2 93.6 %all-gather.6.cloned.1.call-start = ((), (), s32[]{:S(2)}) async-start(), calls=%async_computation.1 | async-start | bytes 2621440 | tf_op jit(solution)/shard_map/all_gather | solution.py:517
  31.1 73.0 %all-gather.8.cloned.1.call-start = ((), (), s32[]{:S(2)}) async-start(), calls=%async_computation.2 | async-start | bytes 5242880 | tf_op jit(solution)/shard_map/all_gather | solution.py:517
  31.9 92.4 %all-gather.10.cloned.1.call-start = ((), (), s32[]{:S(2)}) async-start(), calls=%async_computation.3 | async-start | bytes 2621440 | tf_op jit(solution)/shard_map/all_gather | solution.py:517
  49.0 275.5 %reduce-scatter.2.cloned.1.call-start = ((), (), s32[]{:S(2)}) async-start(), calls=%async_computation.4 | async-start | bytes 4718592 | tf_op jit(solution)/shard_map/reduce_scatter | solution.py:712
  49.8 46.9 %collective-permute-start.14 = (bf16[256,1024]{1,0:T(8,128)(2,1)S(1)}, bf16[256,1024]{1,0:T(8,128)(2,1)}, u32[]{:S(2)}, u32[]{:S(2)}) collective-permute-start(bf16[256,1024]{1,0:T(8,128)(2,1)S(1)} %copy-done.35), channel_id=1, source_target_pairs={{0,1},{1,0},{2,3},{3,2},{4,5},{5,4},{6,7},{7,6},{8,9},{9,8},{10,11... | collective-permute-start | bytes 1572872 | tf_op jit(solution)/shard_map/ppermute | solution.py:396
  66.0 30.7 %collective-permute-start.16 = (bf16[256,1024]{1,0:T(8,128)(2,1)}, bf16[256,1024]{1,0:T(8,128)(2,1)S(1)}, u32[]{:S(2)}, u32[]{:S(2)}) collective-permute-start(bf16[256,1024]{1,0:T(8,128)(2,1)} %collective-permute-done.15.refs_3_), channel_id=1, source_target_pairs={{0,1},{1,0},{2,3},{3,2},{4,5},{5,4},{6,7},{7,6},{8,9},{9,8},{10,11... | collective-permute-start | bytes 1572872 | tf_op jit(solution)/shard_map/ppermute | solution.py:396
  89.4 38.9 %collective-permute-start.22 = (bf16[256,1024]{1,0:T(8,128)(2,1)}, bf16[256,1024]{1,0:T(8,128)(2,1)}, u32[]{:S(2)}, u32[]{:S(2)}) collective-permute-start(bf16[256,1024]{1,0:T(8,128)(2,1)} %get-tuple-element.396), channel_id=1, source_target_pairs={{0,3},{1,2},{2,1},{3,0},{4,7},{5,6},{6,5},{7,4},{8,11},{9,10},{10,... | collective-permute-start | bytes 1572872 | tf_op jit(solution)/shard_map/ppermute | solution.py:396
  95.1 33.2 %collective-permute-start.21 = (bf16[256,1024]{1,0:T(8,128)(2,1)}, bf16[256,1024]{1,0:T(8,128)(2,1)}, u32[]{:S(2)}, u32[]{:S(2)}) collective-permute-start(bf16[256,1024]{1,0:T(8,128)(2,1)} %get-tuple-element.397), channel_id=1, source_target_pairs={{0,2},{1,3},{2,0},{3,1},{4,6},{5,7},{6,4},{7,5},{8,10},{9,11},{10,... | collective-permute-start | bytes 1572872 | tf_op jit(solution)/shard_map/ppermute | solution.py:396
  95.8 32.5 %collective-permute-start.20 = (bf16[256,1024]{1,0:T(8,128)(2,1)}, bf16[256,1024]{1,0:T(8,128)(2,1)}, u32[]{:S(2)}, u32[]{:S(2)}) collective-permute-start(bf16[256,1024]{1,0:T(8,128)(2,1)} %get-tuple-element.398), channel_id=1, source_target_pairs={{0,1},{1,0},{2,3},{3,2},{4,5},{5,4},{6,7},{7,6},{8,9},{9,8},{10,11... | collective-permute-start | bytes 1572872 | tf_op jit(solution)/shard_map/ppermute | solution.py:396
  204.6 171.1 %all-gather.12.cloned.1.call-start = ((), (), s32[]{:S(2)}) async-start(), calls=%async_computation.5 | async-start | bytes 2621440 | tf_op jit(solution)/shard_map/all_gather | solution.py:773
  216.0 37.1 %collective-permute-start.41 = (bf16[256,3072]{1,0:T(8,128)(2,1)}, bf16[256,3072]{1,0:T(8,128)(2,1)}, u32[]{:S(2)}, u32[]{:S(2)}) collective-permute-start(bf16[256,3072]{1,0:T(8,128)(2,1)} %refs_1_.7), channel_id=1, source_target_pairs={{0,2},{1,3},{2,0},{3,1},{4,6},{5,7},{6,4},{7,5},{8,10},{9,11},{10,... | collective-permute-start | bytes 4718600 | tf_op jit(solution)/shard_map/ppermute | solution.py:396
  216.1 37.0 %collective-permute-start.40 = (bf16[256,3072]{1,0:T(8,128)(2,1)}, bf16[256,3072]{1,0:T(8,128)(2,1)}, u32[]{:S(2)}, u32[]{:S(2)}) collective-permute-start(bf16[256,3072]{1,0:T(8,128)(2,1)} %refs_1_.7), channel_id=1, source_target_pairs={{0,1},{1,0},{2,3},{3,2},{4,5},{5,4},{6,7},{7,6},{8,9},{9,8},{10,11... | collective-permute-start | bytes 4718600 | tf_op jit(solution)/shard_map/ppermute | solution.py:396
  268.7 32.6 %collective-permute-start.51 = (bf16[256,1024]{1,0:T(8,128)(2,1)}, bf16[256,1024]{1,0:T(8,128)(2,1)S(1)}, u32[]{:S(2)}, u32[]{:S(2)}) collective-permute-start(bf16[256,1024]{1,0:T(8,128)(2,1)} %fusion.54), channel_id=1, source_target_pairs={{0,2},{1,3},{2,0},{3,1},{4,6},{5,7},{6,4},{7,5},{8,10},{9,11},{10,... | collective-permute-start | bytes 1572872 | tf_op jit(solution)/shard_map/ppermute | solution.py:396
  270.2 42.4 %collective-permute-start.50 = (bf16[256,1024]{1,0:T(8,128)(2,1)}, bf16[256,1024]{1,0:T(8,128)(2,1)S(1)}, u32[]{:S(2)}, u32[]{:S(2)}) collective-permute-start(bf16[256,1024]{1,0:T(8,128)(2,1)} %fusion.53), channel_id=1, source_target_pairs={{0,2},{1,3},{2,0},{3,1},{4,6},{5,7},{6,4},{7,5},{8,10},{9,11},{10,... | collective-permute-start | bytes 1572872 | tf_op jit(solution)/shard_map/ppermute | solution.py:396
  285.4 36.6 %collective-permute-start.49 = (bf16[256,1024]{1,0:T(8,128)(2,1)S(1)}, bf16[256,1024]{1,0:T(8,128)(2,1)S(1)}, u32[]{:S(2)}, u32[]{:S(2)}) collective-permute-start(bf16[256,1024]{1,0:T(8,128)(2,1)S(1)} %copy-done.101), channel_id=1, source_target_pairs={{0,2},{1,3},{2,0},{3,1},{4,6},{5,7},{6,4},{7,5},{8,10},{9,11},{10,... | collective-permute-start | bytes 1572872 | tf_op jit(solution)/shard_map/ppermute | solution.py:396
  286.9 35.1 %collective-permute-start.45 = (bf16[256,768]{1,0:T(8,128)(2,1)S(1)}, bf16[256,768]{1,0:T(8,128)(2,1)S(1)}, u32[]{:S(2)}, u32[]{:S(2)}) collective-permute-start(bf16[256,768]{1,0:T(8,128)(2,1)S(1)} %get-tuple-element.265), channel_id=1, source_target_pairs={{0,4},{4,0},{8,12},{12,8},{1,5},{5,1},{9,13},{13,9},{2,6},{6,2},{1... | collective-permute-start | bytes 1179656 | tf_op jit(solution)/shard_map/ppermute | solution.py:396
  290.1 32.7 %collective-permute-start.46 = (bf16[256,768]{1,0:T(8,128)(2,1)S(1)}, bf16[256,768]{1,0:T(8,128)(2,1)S(1)}, u32[]{:S(2)}, u32[]{:S(2)}) collective-permute-start(bf16[256,768]{1,0:T(8,128)(2,1)S(1)} %get-tuple-element.266), channel_id=1, source_target_pairs={{0,8},{4,12},{8,0},{12,4},{1,9},{5,13},{9,1},{13,5},{2,10},{6,14},... | collective-permute-start | bytes 1179656 | tf_op jit(solution)/shard_map/ppermute | solution.py:396
  324.5 145.0 %all-gather.14.cloned.1.call-start = ((), (), s32[]{:S(2)}) async-start(), calls=%async_computation.6 | async-start | bytes 6291456 | tf_op jit(solution)/shard_map/all_gather | solution.py:794
  382.1 39.7 %collective-permute-start.64 = (bf16[32,7296]{1,0:T(8,128)(2,1)S(1)}, bf16[32,7296]{1,0:T(8,128)(2,1)S(1)}, u32[]{:S(2)}, u32[]{:S(2)}) collective-permute-start(bf16[32,7296]{1,0:T(8,128)(2,1)S(1)} %get-tuple-element.402), channel_id=1, source_target_pairs={{0,8},{4,12},{8,0},{12,4},{1,9},{5,13},{9,1},{13,5},{2,10},{6,14},... | collective-permute-start | bytes 1400840 | tf_op jit(solution)/shard_map/ppermute | solution.py:396
  384.2 38.9 %collective-permute-start.66 = (bf16[128,768]{1,0:T(8,128)(2,1)S(1)}, bf16[128,768]{1,0:T(8,128)(2,1)S(1)}, u32[]{:S(2)}, u32[]{:S(2)}) collective-permute-start(bf16[128,768]{1,0:T(8,128)(2,1)S(1)} %fusion.85), channel_id=1, source_target_pairs={{0,16},{16,0},{1,17},{17,1},{2,18},{18,2},{3,19},{19,3},{4,20},{20... | collective-permute-start | bytes 589832 | tf_op jit(solution)/shard_map/ppermute | solution.py:396
  430.7 38.7 %collective-permute-start.68 = (bf16[32,5120]{1,0:T(8,128)(2,1)S(1)}, bf16[32,5120]{1,0:T(8,128)(2,1)S(1)}, u32[]{:S(2)}, u32[]{:S(2)}) collective-permute-start(bf16[32,5120]{1,0:T(8,128)(2,1)S(1)} %slice.527.refs_1_), channel_id=1, source_target_pairs={{0,8},{4,12},{8,0},{12,4},{1,9},{5,13},{9,1},{13,5},{2,10},{6,14},... | collective-permute-start | bytes 983048 | tf_op jit(solution)/shard_map/ppermute | solution.py:396
  434.8 34.6 %collective-permute-start.67 = (bf16[32,5120]{1,0:T(8,128)(2,1)S(1)}, bf16[32,5120]{1,0:T(8,128)(2,1)S(1)}, u32[]{:S(2)}, u32[]{:S(2)}) collective-permute-start(bf16[32,5120]{1,0:T(8,128)(2,1)S(1)} %slice.527.refs_1_), channel_id=1, source_target_pairs={{0,4},{4,0},{8,12},{12,8},{1,5},{5,1},{9,13},{13,9},{2,6},{6,2},{1... | collective-permute-start | bytes 983048 | tf_op jit(solution)/shard_map/ppermute | solution.py:396
  469.5 49.6 %collective-permute-start.74 = (bf16[128,5120]{1,0:T(8,128)(2,1)S(1)}, bf16[128,5120]{1,0:T(8,128)(2,1)}, u32[]{:S(2)}, u32[]{:S(2)}) collective-permute-start(bf16[128,5120]{1,0:T(8,128)(2,1)S(1)} %shard_map.240.own_ref), channel_id=1, source_target_pairs={{0,16},{16,0},{1,17},{17,1},{2,18},{18,2},{3,19},{19,3},{4,20},{20... | collective-permute-start | bytes 3932168 | tf_op jit(solution)/shard_map/ppermute | solution.py:396
  471.1 44.9 %collective-permute-start.73 = (bf16[512,768]{1,0:T(8,128)(2,1)S(1)}, bf16[512,768]{1,0:T(8,128)(2,1)}, u32[]{:S(2)}, u32[]{:S(2)}) collective-permute-start(bf16[512,768]{1,0:T(8,128)(2,1)S(1)} %shard_map.241.own_ref), channel_id=1, source_target_pairs={{0,16},{16,0},{1,17},{17,1},{2,18},{18,2},{3,19},{19,3},{4,20},{20... | collective-permute-start | bytes 2359304 | tf_op jit(solution)/shard_map/ppermute | solution.py:396
  (195 other events, 1911.0 us)
Sparse Core Ops, SparseCore 0:
  31.2 21.0 all-gather.5
  53.8 34.7 all-gather.7
  90.2 33.9 all-gather.9
  204.7 103.5 reduce-scatter.1
  324.6 50.9 all-gather.11
  377.1 57.9 all-gather.13

commit v3 on v2

--- a/solution.py
+++ b/solution.py
@@ -517,7 +517,7 @@
         return lax.all_gather(shard, "fsdp", axis=0, tiled=True)
 
     w_ckv = gather(cross_kv)
-    w_cq, w_co = gather(after(cross_q, seen[0])), gather(after(cross_out, seen[0]))
+    w_cq, w_co = gather(cross_q), gather(after(cross_out, seen[0]))
     ff_later = after(ff_in, x_moving[0])
     ff_pieces = exchanged(
         lambda owner: lax.dynamic_slice_in_dim(ff_later, owner * ff_width, ff_width, 1), "fsdp"

time: 535 us -> 531 us (level)
  waiting for transfers between devices: 234 us -> 217 us
  starting transfers between devices: 67.7 us -> 83.6 us
    ppermute x72, starting transfers between devices: 62.6 us -> 78.6 us  [swap(): lax.ppermute(value, axis, [(i, i ^ mask) for i in range(size_of[axis])])]
    all_gather x3, waiting for transfers between devices: 8.83 us -> 0.02 us  [gather(): return lax.all_gather(shard, 'fsdp', axis=0, tiled=True)]
    ppermute x72, waiting for transfers between devices: 193 us -> 185 us  [swap(): lax.ppermute(value, axis, [(i, i ^ mask) for i in range(size_of[axis])])]
    unnamed x286 -> x272, local copies, waits for them, and re-layouts: 27.4 us -> 24.6 us
  transfers between devices with their start and end apart: 84 -> 84, of which waited for: 39 -> 35; matrix products, arithmetic and copies ran while one was open for 23% -> 23% of each run, Pallas kernels for 10% -> 10%
where the time goes in v3:
time: 531 us; the launch traced here: 527 us
  waiting for transfers between devices  217 us (41%)
  starting transfers between devices  83.6 us (16%)
  matrix products  81.1 us (15%)
  Pallas kernels  55.1 us (10%)
  local copies, waits for them, and re-layouts  47.9 us (9%)
  other arithmetic  26.3 us (5%)
  between operations  16.1 us (3%)
    ppermute x72, waiting for transfers between devices, swap(): lax.ppermute(value, axis, [(i, i ^ mask) for i in range(size_of[axis])])  185 us
    ppermute x72, starting transfers between devices, swap(): lax.ppermute(value, axis, [(i, i ^ mask) for i in range(size_of[axis])])  78.6 us
    dot_general x26, matrix products, dot_rows(): lax.dot_general(left, right, (((0,), (0,)), ((), ())), preferred_element_...  40.8 us
    ppermute x6, waiting for transfers between devices, local(): lax.ppermute(v, 'ctx', [(i, (i + 1) % C) for i in range(C)])  27.9 us
    unnamed x272, local copies, waits for them, and re-layouts  24.6 us
    dot_general x9, matrix products, dot(): return jnp.dot(left, right, preferred_element_type=F32)  21.6 us
    dot_general x13, matrix products, dot_cols(): lax.dot_general(left, right, (((1,), (1,)), ((), ())), preferred_element_...  18.7 us
    pallas_call x19, Pallas kernels, moved(): pl.pallas_call(kernel, in_specs=[SMEM] * len(scalars) + [IN_VMEM] * len(v...  18.7 us
  transfers between devices with their start and end apart: 84, of which 35 were waited for; matrix products, arithmetic and copies ran while one was open for 23% of the time, Pallas kernels for 10%

profile of v3, /device:TPU:0, one launch (start us, length us, event | category | flops | bytes accessed | tf_op | source)
XLA Modules:
  0.0 527.0 jit_solution(6145242219341834814)
XLA Ops:
  33.1 9.3 %collective-permute-done.6.refs_7_ = bf16[128,1024]{1,0:T(8,128)(2,1)} collective-permute-done((bf16[128,1024]{1,0:T(8,128)(2,1)}, bf16[128,1024]{1,0:T(8,128)(2,1)}, u32[]{:S(2)}, u32[]{:S(2)}) %collective-permute-start.6) | collective-permute-done | bytes 262176 | tf_op jit(solution)/shard_map/ppermute | solution.py:489
  65.1 8.2 %collective-permute-done.15.refs_3_ = bf16[256,1024]{1,0:T(8,128)(2,1)} collective-permute-done((bf16[256,1024]{1,0:T(8,128)(2,1)S(1)}, bf16[256,1024]{1,0:T(8,128)(2,1)}, u32[]{:S(2)}, u32[]{:S(2)}) %collective-permute-start.15) | collective-permute-done | bytes 524320 | tf_op jit(solution)/shard_map/ppermute | solution.py:396
  73.4 7.7 %shard_map.222 = (bf16[1024,256]{1,0:T(8,128)(2,1)S(1)}, f32[256,1024]{1,0:T(8,128)S(1)}, f32[8,1024]{1,0:T(8,128)S(1)}) custom-call(bf16[1024,768]{1,0:T(8,128)(2,1)S(1)} %convolution_convert_fusion.1.q_ref.k_ref.v_ref, bf16[1024,768]{1,0:T(8,128)(2,1)S(1)} %convolution_convert_fusion.1.q_ref.k_ref.v_ref, ...), custom_call_target="tpu_custom_call" | custom-call | flops 1073741824 | bytes 4194304 | tf_op jit(solution)/shard_map/pallas_call | solution.py:210
  89.3 6.5 %collective-permute-start.13 = (bf16[256,256]{1,0:T(8,128)(2,1)S(1)}, bf16[256,256]{1,0:T(8,128)(2,1)S(1)}, u32[]{:S(2)}, u32[]{:S(2)}) collective-permute-start(bf16[256,256]{1,0:T(8,128)(2,1)S(1)} %get-tuple-element.201), channel_id=1, source_target_pairs={{0,12},{4,8},{8,4},{12,0},{1,13},{5,9},{9,5},{13,1},{2,14},{6,10},... | collective-permute-start | bytes 393224 | tf_op jit(solution)/shard_map/ppermute | solution.py:396
  97.3 6.5 %collective-permute-done.13.refs_3_ = bf16[256,256]{1,0:T(8,128)(2,1)S(1)} collective-permute-done((bf16[256,256]{1,0:T(8,128)(2,1)S(1)}, bf16[256,256]{1,0:T(8,128)(2,1)S(1)}, u32[]{:S(2)}, u32[]{:S(2)}) %collective-permute-start.13) | collective-permute-done | bytes 131104 | tf_op jit(solution)/shard_map/ppermute | solution.py:396
  116.4 5.8 %shard_map.226 = (bf16[256,1024]{1,0:T(8,128)(2,1)S(1)}, f32[1024,256]{1,0:T(8,128)S(1)}, f32[32,256]{1,0:T(8,128)S(1)}) custom-call(bf16[256,1024]{1,0:T(8,128)(2,1)S(1)} %copy-done.30, bf16[256,2048]{1,0:T(8,128)(2,1)S(1)} %convolution_convert_fusion.k_ref.v_ref, bf16[256,2048]{1,0:T(8,128)(2,1)S(1)} %convolution_convert_fusion.k_ref.v_ref), custom_call_target="tpu_custom_call" | custom-call | flops 268435456 | bytes 4194304 | tf_op jit(solution)/shard_map/pallas_call | solution.py:210
  134.4 7.5 %collective-permute-done.23 = bf16[256,1024]{1,0:T(8,128)(2,1)S(1)} collective-permute-done((bf16[256,1024]{1,0:T(8,128)(2,1)S(1)}, bf16[256,1024]{1,0:T(8,128)(2,1)S(1)}, u32[]{:S(2)}, u32[]{:S(2)}) %collective-permute-start.23) | collective-permute-done | bytes 524320 | tf_op jit(solution)/shard_map/ppermute | solution.py:396
  172.9 10.2 %collective-permute-done.29 = bf16[256,1024]{1,0:T(8,128)(2,1)S(1)} collective-permute-done((bf16[256,1024]{1,0:T(8,128)(2,1)S(1)}, bf16[256,1024]{1,0:T(8,128)(2,1)S(1)}, u32[]{:S(2)}, u32[]{:S(2)}) %collective-permute-start.29) | collective-permute-done | bytes 524320 | tf_op jit(solution)/shard_map/ppermute | solution.py:396
  230.0 8.9 %collective-permute-done.34 = bf16[256,256]{1,0:T(8,128)(2,1)} collective-permute-done((bf16[256,256]{1,0:T(8,128)(2,1)}, bf16[256,256]{1,0:T(8,128)(2,1)}, u32[]{:S(2)}, u32[]{:S(2)}) %collective-permute-start.34) | collective-permute-done | bytes 131104 | tf_op jit(solution)/shard_map/ppermute | solution.py:396
  242.8 9.9 %collective-permute-done.41.refs_3_ = bf16[256,3072]{1,0:T(8,128)(2,1)} collective-permute-done((bf16[256,3072]{1,0:T(8,128)(2,1)}, bf16[256,3072]{1,0:T(8,128)(2,1)}, u32[]{:S(2)}, u32[]{:S(2)}) %collective-permute-start.41) | collective-permute-done | bytes 1572896 | tf_op jit(solution)/shard_map/ppermute | solution.py:396
  272.1 10.2 %shard_map.235 = (bf16[1024,256]{1,0:T(8,128)(2,1)S(1)}, bf16[1024,256]{1,0:T(8,128)(2,1)S(1)}, bf16[1024,256]{1,0:T(8,128)(2,1)S(1)}) custom-call(bf16[1024,768]{1,0:T(8,128)(2,1)S(1)} %copy-done.49, bf16[1024,768]{1,0:T(8,128)(2,1)S(1)} %copy-done.49, bf16[1024,768]{1,0:T(8,128)(2,1)S(1)} %copy-done.49, bf16[1024,256]{1,0:T(8,128)(2,1)S(1)} %shard_map.234.do_ref, ...), custom_call_target="tpu_custom_call" | custom-call | flops 2684354560 | bytes 6291456 | tf_op jit(solution)/shard_map/pallas_call | solution.py:231
  289.8 9.5 %collective-permute-done.51 = bf16[256,1024]{1,0:T(8,128)(2,1)S(1)} collective-permute-done((bf16[256,1024]{1,0:T(8,128)(2,1)}, bf16[256,1024]{1,0:T(8,128)(2,1)S(1)}, u32[]{:S(2)}, u32[]{:S(2)}) %collective-permute-start.51) | collective-permute-done | bytes 524320 | tf_op jit(solution)/shard_map/ppermute | solution.py:396
  302.1 6.1 %shard_map.237 = bf16[1024,3072]{1,0:T(8,128)(2,1)} custom-call(s32[1]{0:T(128)} %bitcast.4.refs_0_.at_ref, bf16[256,3072]{1,0:T(8,128)(2,1)} %refs_1_.7, bf16[256,3072]{1,0:T(8,128)(2,1)} %collective-permute-done.40.refs_2_, bf16[256,3072]{1,0:T(8,128)(2,1)} %collective-permute-done.41.refs_3_, bf16[256,3072]{1,0:T(8,128)(2,1)} %collective-permute-done.42.refs_4_), custom_call_target="tpu_custom_call" | custom-call | bytes 12582912 | tf_op jit(solution)/shard_map/pallas_call | solution.py:255
  312.0 8.0 %collective-permute-done.49 = bf16[256,1024]{1,0:T(8,128)(2,1)S(1)} collective-permute-done((bf16[256,1024]{1,0:T(8,128)(2,1)S(1)}, bf16[256,1024]{1,0:T(8,128)(2,1)S(1)}, u32[]{:S(2)}, u32[]{:S(2)}) %collective-permute-start.49) | collective-permute-done | bytes 524320 | tf_op jit(solution)/shard_map/ppermute | solution.py:396
  342.0 11.6 %collective-permute-done.58 = bf16[128,1024]{1,0:T(8,128)(2,1)} collective-permute-done((bf16[128,1024]{1,0:T(8,128)(2,1)}, bf16[128,1024]{1,0:T(8,128)(2,1)}, u32[]{:S(2)}, u32[]{:S(2)}) %collective-permute-start.58) | collective-permute-done | bytes 262176 | tf_op jit(solution)/shard_map/ppermute | solution.py:396
  383.4 8.1 %collective-permute-done.62 = bf16[32,7296]{1,0:T(8,128)(2,1)S(1)} collective-permute-done((bf16[32,7296]{1,0:T(8,128)(2,1)S(1)}, bf16[32,7296]{1,0:T(8,128)(2,1)S(1)}, u32[]{:S(2)}, u32[]{:S(2)}) %collective-permute-start.62) | collective-permute-done | bytes 466976 | tf_op jit(solution)/shard_map/ppermute | solution.py:396
  391.6 10.2 %collective-permute-done.65 = bf16[32,7296]{1,0:T(8,128)(2,1)S(1)} collective-permute-done((bf16[32,7296]{1,0:T(8,128)(2,1)S(1)}, bf16[32,7296]{1,0:T(8,128)(2,1)S(1)}, u32[]{:S(2)}, u32[]{:S(2)}) %collective-permute-start.65) | collective-permute-done | bytes 466976 | tf_op jit(solution)/shard_map/ppermute | solution.py:396
  401.7 17.3 %collective-permute-done.64 = bf16[32,7296]{1,0:T(8,128)(2,1)S(1)} collective-permute-done((bf16[32,7296]{1,0:T(8,128)(2,1)S(1)}, bf16[32,7296]{1,0:T(8,128)(2,1)S(1)}, u32[]{:S(2)}, u32[]{:S(2)}) %collective-permute-start.64) | collective-permute-done | bytes 466976 | tf_op jit(solution)/shard_map/ppermute | solution.py:396
  432.0 8.8 %collective-permute-start.67 = (bf16[32,5120]{1,0:T(8,128)(2,1)S(1)}, bf16[32,5120]{1,0:T(8,128)(2,1)S(1)}, u32[]{:S(2)}, u32[]{:S(2)}) collective-permute-start(bf16[32,5120]{1,0:T(8,128)(2,1)S(1)} %slice.527.refs_1_), channel_id=1, source_target_pairs={{0,4},{4,0},{8,12},{12,8},{1,5},{5,1},{9,13},{13,9},{2,6},{6,2},{1... | collective-permute-start | bytes 983048 | tf_op jit(solution)/shard_map/ppermute | solution.py:396
  446.4 8.7 %collective-permute-done.71.refs_3_ = bf16[128,768]{1,0:T(8,128)(2,1)S(1)} collective-permute-done((bf16[128,768]{1,0:T(8,128)(2,1)S(1)}, bf16[128,768]{1,0:T(8,128)(2,1)S(1)}, u32[]{:S(2)}, u32[]{:S(2)}) %collective-permute-start.71) | collective-permute-done | bytes 196640 | tf_op jit(solution)/shard_map/ppermute | solution.py:396
  455.1 11.9 %collective-permute-done.68.refs_3_ = bf16[32,5120]{1,0:T(8,128)(2,1)S(1)} collective-permute-done((bf16[32,5120]{1,0:T(8,128)(2,1)S(1)}, bf16[32,5120]{1,0:T(8,128)(2,1)S(1)}, u32[]{:S(2)}, u32[]{:S(2)}) %collective-permute-start.68) | collective-permute-done | bytes 327712 | tf_op jit(solution)/shard_map/ppermute | solution.py:396
  482.6 6.9 %collective-permute-done.76.refs_2_ = bf16[256,1024]{1,0:T(8,128)(2,1)S(1)} collective-permute-done((bf16[256,1024]{1,0:T(8,128)(2,1)}, bf16[256,1024]{1,0:T(8,128)(2,1)S(1)}, u32[]{:S(2)}, u32[]{:S(2)}) %collective-permute-start.76) | collective-permute-done | bytes 524320 | tf_op jit(solution)/shard_map/ppermute | solution.py:396
  490.3 6.4 %collective-permute-done.77.refs_3_ = bf16[256,1024]{1,0:T(8,128)(2,1)} collective-permute-done((bf16[256,1024]{1,0:T(8,128)(2,1)}, bf16[256,1024]{1,0:T(8,128)(2,1)}, u32[]{:S(2)}, u32[]{:S(2)}) %collective-permute-start.77) | collective-permute-done | bytes 524320 | tf_op jit(solution)/shard_map/ppermute | solution.py:396
  501.4 11.6 %collective-permute-done.73.other_ref = bf16[512,768]{1,0:T(8,128)(2,1)} collective-permute-done((bf16[512,768]{1,0:T(8,128)(2,1)S(1)}, bf16[512,768]{1,0:T(8,128)(2,1)}, u32[]{:S(2)}, u32[]{:S(2)}) %collective-permute-start.73) | collective-permute-done | bytes 786464 | tf_op jit(solution)/shard_map/ppermute | solution.py:396
  (570 shorter events, 295.2 us)
Async XLA Ops:
  7.2 102.2 %all-gather.6.cloned.1.call-start = ((), (), s32[]{:S(2)}) async-start(), calls=%async_computation.1 | async-start | bytes 2621440 | tf_op jit(solution)/shard_map/all_gather | solution.py:517
  7.9 104.8 %all-gather.8.cloned.1.call-start = ((), (), s32[]{:S(2)}) async-start(), calls=%async_computation.2 | async-start | bytes 5242880 | tf_op jit(solution)/shard_map/all_gather | solution.py:517
  8.7 115.3 %all-gather.10.cloned.1.call-start = ((), (), s32[]{:S(2)}) async-start(), calls=%async_computation.3 | async-start | bytes 2621440 | tf_op jit(solution)/shard_map/all_gather | solution.py:517
  48.1 274.4 %reduce-scatter.2.cloned.1.call-start = ((), (), s32[]{:S(2)}) async-start(), calls=%async_computation.4 | async-start | bytes 4718592 | tf_op jit(solution)/shard_map/reduce_scatter | solution.py:712
  48.9 56.5 %collective-permute-start.14 = (bf16[256,1024]{1,0:T(8,128)(2,1)S(1)}, bf16[256,1024]{1,0:T(8,128)(2,1)}, u32[]{:S(2)}, u32[]{:S(2)}) collective-permute-start(bf16[256,1024]{1,0:T(8,128)(2,1)S(1)} %copy-done.35), channel_id=1, source_target_pairs={{0,1},{1,0},{2,3},{3,2},{4,5},{5,4},{6,7},{7,6},{8,9},{9,8},{10,11... | collective-permute-start | bytes 1572872 | tf_op jit(solution)/shard_map/ppermute | solution.py:396
  73.4 32.1 %collective-permute-start.16 = (bf16[256,1024]{1,0:T(8,128)(2,1)}, bf16[256,1024]{1,0:T(8,128)(2,1)S(1)}, u32[]{:S(2)}, u32[]{:S(2)}) collective-permute-start(bf16[256,1024]{1,0:T(8,128)(2,1)} %collective-permute-done.15.refs_3_), channel_id=1, source_target_pairs={{0,1},{1,0},{2,3},{3,2},{4,5},{5,4},{6,7},{7,6},{8,9},{9,8},{10,11... | collective-permute-start | bytes 1572872 | tf_op jit(solution)/shard_map/ppermute | solution.py:396
  97.2 32.1 %collective-permute-start.22 = (bf16[256,1024]{1,0:T(8,128)(2,1)}, bf16[256,1024]{1,0:T(8,128)(2,1)}, u32[]{:S(2)}, u32[]{:S(2)}) collective-permute-start(bf16[256,1024]{1,0:T(8,128)(2,1)} %get-tuple-element.394), channel_id=1, source_target_pairs={{0,3},{1,2},{2,1},{3,0},{4,7},{5,6},{6,5},{7,4},{8,11},{9,10},{10,... | collective-permute-start | bytes 1572872 | tf_op jit(solution)/shard_map/ppermute | solution.py:396
  205.5 168.0 %all-gather.12.cloned.1.call-start = ((), (), s32[]{:S(2)}) async-start(), calls=%async_computation.5 | async-start | bytes 2621440 | tf_op jit(solution)/shard_map/all_gather | solution.py:773
  215.6 37.1 %collective-permute-start.41 = (bf16[256,3072]{1,0:T(8,128)(2,1)}, bf16[256,3072]{1,0:T(8,128)(2,1)}, u32[]{:S(2)}, u32[]{:S(2)}) collective-permute-start(bf16[256,3072]{1,0:T(8,128)(2,1)} %refs_1_.7), channel_id=1, source_target_pairs={{0,2},{1,3},{2,0},{3,1},{4,6},{5,7},{6,4},{7,5},{8,10},{9,11},{10,... | collective-permute-start | bytes 4718600 | tf_op jit(solution)/shard_map/ppermute | solution.py:396
  217.0 35.7 %collective-permute-start.40 = (bf16[256,3072]{1,0:T(8,128)(2,1)}, bf16[256,3072]{1,0:T(8,128)(2,1)}, u32[]{:S(2)}, u32[]{:S(2)}) collective-permute-start(bf16[256,3072]{1,0:T(8,128)(2,1)} %refs_1_.7), channel_id=1, source_target_pairs={{0,1},{1,0},{2,3},{3,2},{4,5},{5,4},{6,7},{7,6},{8,9},{9,8},{10,11... | collective-permute-start | bytes 4718600 | tf_op jit(solution)/shard_map/ppermute | solution.py:396
  266.7 32.6 %collective-permute-start.51 = (bf16[256,1024]{1,0:T(8,128)(2,1)}, bf16[256,1024]{1,0:T(8,128)(2,1)S(1)}, u32[]{:S(2)}, u32[]{:S(2)}) collective-permute-start(bf16[256,1024]{1,0:T(8,128)(2,1)} %fusion.54), channel_id=1, source_target_pairs={{0,2},{1,3},{2,0},{3,1},{4,6},{5,7},{6,4},{7,5},{8,10},{9,11},{10,... | collective-permute-start | bytes 1572872 | tf_op jit(solution)/shard_map/ppermute | solution.py:396
  268.2 42.3 %collective-permute-start.50 = (bf16[256,1024]{1,0:T(8,128)(2,1)}, bf16[256,1024]{1,0:T(8,128)(2,1)S(1)}, u32[]{:S(2)}, u32[]{:S(2)}) collective-permute-start(bf16[256,1024]{1,0:T(8,128)(2,1)} %fusion.53), channel_id=1, source_target_pairs={{0,2},{1,3},{2,0},{3,1},{4,6},{5,7},{6,4},{7,5},{8,10},{9,11},{10,... | collective-permute-start | bytes 1572872 | tf_op jit(solution)/shard_map/ppermute | solution.py:396
  283.4 36.6 %collective-permute-start.49 = (bf16[256,1024]{1,0:T(8,128)(2,1)S(1)}, bf16[256,1024]{1,0:T(8,128)(2,1)S(1)}, u32[]{:S(2)}, u32[]{:S(2)}) collective-permute-start(bf16[256,1024]{1,0:T(8,128)(2,1)S(1)} %copy-done.95), channel_id=1, source_target_pairs={{0,2},{1,3},{2,0},{3,1},{4,6},{5,7},{6,4},{7,5},{8,10},{9,11},{10,... | collective-permute-start | bytes 1572872 | tf_op jit(solution)/shard_map/ppermute | solution.py:396
  284.8 35.1 %collective-permute-start.45 = (bf16[256,768]{1,0:T(8,128)(2,1)S(1)}, bf16[256,768]{1,0:T(8,128)(2,1)S(1)}, u32[]{:S(2)}, u32[]{:S(2)}) collective-permute-start(bf16[256,768]{1,0:T(8,128)(2,1)S(1)} %get-tuple-element.263), channel_id=1, source_target_pairs={{0,4},{4,0},{8,12},{12,8},{1,5},{5,1},{9,13},{13,9},{2,6},{6,2},{1... | collective-permute-start | bytes 1179656 | tf_op jit(solution)/shard_map/ppermute | solution.py:396
  288.7 32.1 %collective-permute-start.46 = (bf16[256,768]{1,0:T(8,128)(2,1)S(1)}, bf16[256,768]{1,0:T(8,128)(2,1)S(1)}, u32[]{:S(2)}, u32[]{:S(2)}) collective-permute-start(bf16[256,768]{1,0:T(8,128)(2,1)S(1)} %get-tuple-element.264), channel_id=1, source_target_pairs={{0,8},{4,12},{8,0},{12,4},{1,9},{5,13},{9,1},{13,5},{2,10},{6,14},... | collective-permute-start | bytes 1179656 | tf_op jit(solution)/shard_map/ppermute | solution.py:396
  322.5 144.6 %all-gather.14.cloned.1.call-start = ((), (), s32[]{:S(2)}) async-start(), calls=%async_computation.6 | async-start | bytes 6291456 | tf_op jit(solution)/shard_map/all_gather | solution.py:794
  380.0 39.0 %collective-permute-start.64 = (bf16[32,7296]{1,0:T(8,128)(2,1)S(1)}, bf16[32,7296]{1,0:T(8,128)(2,1)S(1)}, u32[]{:S(2)}, u32[]{:S(2)}) collective-permute-start(bf16[32,7296]{1,0:T(8,128)(2,1)S(1)} %get-tuple-element.400), channel_id=1, source_target_pairs={{0,8},{4,12},{8,0},{12,4},{1,9},{5,13},{9,1},{13,5},{2,10},{6,14},... | collective-permute-start | bytes 1400840 | tf_op jit(solution)/shard_map/ppermute | solution.py:396
  381.8 38.6 %collective-permute-start.66 = (bf16[128,768]{1,0:T(8,128)(2,1)S(1)}, bf16[128,768]{1,0:T(8,128)(2,1)S(1)}, u32[]{:S(2)}, u32[]{:S(2)}) collective-permute-start(bf16[128,768]{1,0:T(8,128)(2,1)S(1)} %fusion.85), channel_id=1, source_target_pairs={{0,16},{16,0},{1,17},{17,1},{2,18},{18,2},{3,19},{19,3},{4,20},{20... | collective-permute-start | bytes 589832 | tf_op jit(solution)/shard_map/ppermute | solution.py:396
  424.1 30.9 %collective-permute-start.71 = (bf16[128,768]{1,0:T(8,128)(2,1)S(1)}, bf16[128,768]{1,0:T(8,128)(2,1)S(1)}, u32[]{:S(2)}, u32[]{:S(2)}) collective-permute-start(bf16[128,768]{1,0:T(8,128)(2,1)S(1)} %fusion.86.refs_1_), channel_id=1, source_target_pairs={{0,8},{4,12},{8,0},{12,4},{1,9},{5,13},{9,1},{13,5},{2,10},{6,14},... | collective-permute-start | bytes 589832 | tf_op jit(solution)/shard_map/ppermute | solution.py:396
  424.2 30.9 %collective-permute-start.70 = (bf16[128,768]{1,0:T(8,128)(2,1)S(1)}, bf16[128,768]{1,0:T(8,128)(2,1)S(1)}, u32[]{:S(2)}, u32[]{:S(2)}) collective-permute-start(bf16[128,768]{1,0:T(8,128)(2,1)S(1)} %fusion.86.refs_1_), channel_id=1, source_target_pairs={{0,4},{4,0},{8,12},{12,8},{1,5},{5,1},{9,13},{13,9},{2,6},{6,2},{1... | collective-permute-start | bytes 589832 | tf_op jit(solution)/shard_map/ppermute | solution.py:396
  428.5 38.5 %collective-permute-start.68 = (bf16[32,5120]{1,0:T(8,128)(2,1)S(1)}, bf16[32,5120]{1,0:T(8,128)(2,1)S(1)}, u32[]{:S(2)}, u32[]{:S(2)}) collective-permute-start(bf16[32,5120]{1,0:T(8,128)(2,1)S(1)} %slice.527.refs_1_), channel_id=1, source_target_pairs={{0,8},{4,12},{8,0},{12,4},{1,9},{5,13},{9,1},{13,5},{2,10},{6,14},... | collective-permute-start | bytes 983048 | tf_op jit(solution)/shard_map/ppermute | solution.py:396
  432.0 35.0 %collective-permute-start.67 = (bf16[32,5120]{1,0:T(8,128)(2,1)S(1)}, bf16[32,5120]{1,0:T(8,128)(2,1)S(1)}, u32[]{:S(2)}, u32[]{:S(2)}) collective-permute-start(bf16[32,5120]{1,0:T(8,128)(2,1)S(1)} %slice.527.refs_1_), channel_id=1, source_target_pairs={{0,4},{4,0},{8,12},{12,8},{1,5},{5,1},{9,13},{13,9},{2,6},{6,2},{1... | collective-permute-start | bytes 983048 | tf_op jit(solution)/shard_map/ppermute | solution.py:396
  467.1 48.8 %collective-permute-start.74 = (bf16[128,5120]{1,0:T(8,128)(2,1)S(1)}, bf16[128,5120]{1,0:T(8,128)(2,1)}, u32[]{:S(2)}, u32[]{:S(2)}) collective-permute-start(bf16[128,5120]{1,0:T(8,128)(2,1)S(1)} %shard_map.240.own_ref), channel_id=1, source_target_pairs={{0,16},{16,0},{1,17},{17,1},{2,18},{18,2},{3,19},{19,3},{4,20},{20... | collective-permute-start | bytes 3932168 | tf_op jit(solution)/shard_map/ppermute | solution.py:396
  468.6 44.3 %collective-permute-start.73 = (bf16[512,768]{1,0:T(8,128)(2,1)S(1)}, bf16[512,768]{1,0:T(8,128)(2,1)}, u32[]{:S(2)}, u32[]{:S(2)}) collective-permute-start(bf16[512,768]{1,0:T(8,128)(2,1)S(1)} %shard_map.241.own_ref), channel_id=1, source_target_pairs={{0,16},{16,0},{1,17},{17,1},{2,18},{18,2},{3,19},{19,3},{4,20},{20... | collective-permute-start | bytes 2359304 | tf_op jit(solution)/shard_map/ppermute | solution.py:396
  (188 other events, 1886.5 us)
Sparse Core Ops, SparseCore 0:
  9.6 25.2 all-gather.5
  36.5 47.1 all-gather.7
  85.2 29.1 all-gather.9
  205.6 100.0 reduce-scatter.1
  322.6 50.8 all-gather.11
  375.0 57.6 all-gather.13
